TPU v7x, 128 devices: a whole 4x4x4 slice. The times are simulated.
128 devices in a mesh: ctx: 16 (over x_lo, y, core), ch: 8 (over z, x_hi).
Axes of the slice: x: 4 (x_hi: 2, x_lo: 2; x = x_hi * 2 + x_lo), y: 4, z: 4, core: 2. Of those that a mesh axis runs over, the one named last changes fastest.
Arguments:
- hidden: bfloat16 [8192, 4096], P('ctx', 'ch'), may hold values from -6 to 6
- norm_gain: float32 [2, 4096], replicated, may hold values from 0.5 to 2
- in_weight: bfloat16 [2, 4096, 3, 4096], P(None, 'ctx', None, 'ch'), may hold values from -0.09375 to 0.09375
- feat_filter: float32 [2, 3, 3, 4096], P(None, None, None, 'ch'), may hold values from -3 to 3
- se_filter: float32 [7, 4096], P(None, 'ch'), may hold values from -2 to 2
- mr_filter: float32 [128, 4096], P(None, 'ch'), may hold values from -0.5 to 0.5
- skip_gain: float32 [2, 4096], P(None, 'ch'), may hold values from -1 to 1
- out_weight: bfloat16 [2, 4096, 4096], P(None, 'ch', 'ctx'), may hold values from -0.125 to 0.125
Outputs:
- result: bfloat16 [8192, 4096], P('ctx', 'ch')
All inputs are finite; a program needn't handle non-finite values.
Results may differ from a plain program's by a relative error of at most 0.04.
Values may be sent and summed in bfloat16 or wider, within the bound.
No kernel may reach another device: no remote copies, remote signals or barrier semaphores. Data moves between devices by JAX's collectives and lax.ppermute only.
A program may use at most 128 MiB of HBM per device.

v0:
```python
import functools

import jax
import jax.numpy as jnp
import numpy as np
from jax import lax
from jax.experimental.layout import Layout, with_layout_constraint
from jax.experimental import pallas as pl
from jax.experimental.pallas import tpu as pltpu
from jax.sharding import Mesh, PartitionSpec as P

AXES = ("xl", "y", "core", "z", "xh")
HALF = 256
CUT = 1280
LANES = 128


def shift(value, axis, by):
    size = lax.axis_size(axis)
    return lax.ppermute(value, axis, [(i, (i + by) % size) for i in range(size)])


def swap(value):
    moved = lax.ppermute(value, ("core", "xh"), [(1, 2), (2, 1)])
    same = lax.axis_index("core") == lax.axis_index("xh")
    return jnp.where(same, value, moved)


def from_behind(value, axes):
    return lax.ppermute(value, axes, [(i, i + 1) for i in range(15)])


def by_rows(value):
    return with_layout_constraint(value, Layout(major_to_minor=tuple(range(value.ndim))))


def after(value, *others):
    return lax.optimization_barrier((value, *others))[0]


def together(*values):
    return lax.optimization_barrier(values)


def fetch(moves, sources, target, index_ref, semaphores):
    copies = []
    for number, (source, lead, lane, width, slot, other, by_rows, *fixed) in enumerate(moves):
        block = fixed[0] * 256 if slot is None else pl.multiple_of(index_ref[slot] * 256, 256)
        ref = sources[source]
        if lead is not None:
            ref = ref.at[lead]
        if by_rows:
            piece = target.at[pl.ds(block, 256), other : other + width]
        else:
            piece = target.at[other : other + ref.shape[0], pl.ds(block, 256)]
        copies.append(pltpu.make_async_copy(ref.at[:, lane : lane + width], piece, semaphores.at[number]))
    return copies


def norm_pieces(loads, places, raw, gain_ref, normed, squares):
    squares[...] = jnp.zeros_like(squares)
    for load, (j, start, count), place in zip(loads, pieces_of(len(loads)), places):
        load.wait()
        lanes = pl.ds(pl.multiple_of(place * 512, 512), 512)
        gain = gain_ref[pl.ds(place, 1), :]

        @pl.loop(0, count // 64)
        def _(step):
            rows = pl.ds(pl.multiple_of(start + step * 64, 64), 64)
            x = raw[j, rows, :].astype(jnp.float32)
            normed[rows, lanes] = (x * gain).astype(jnp.bfloat16)
            q = x * x
            squares[rows, :] += (q[:, :128] + q[:, 128:256]) + (q[:, 256:384] + q[:, 384:])

    squares[:, :1] = lax.rsqrt(jnp.sum(squares[...], axis=1, keepdims=True) * (1.0 / 4096) + 1e-06)


def pieces_of(count):
    rows = 8 * 2 * HALF // count
    return [(j % 8, j // 8 * rows, rows) for j in range(count)]


def in_kernel(moves, sources, halo, index_ref, place_ref, gain_ref, *refs):
    xs, refs = refs[:sources], refs[sources:]
    count = 1 + max(m[0] for m in moves)
    ws, refs = refs[:count], refs[count:]
    out_refs, (tail_ref, raw, normed, weights, squares, x_sems, w_sems) = refs[:2], refs[2:]
    xs = [xs[0].at[j] for j in range(8)] if sources == 1 else xs
    loads = [
        pltpu.make_async_copy(x, raw.at[j, start : start + rows], x_sems.at[number])
        for number, (x, (j, start, rows)) in enumerate(zip(xs, pieces_of(len(xs))))
    ]
    copies = fetch(moves, ws, weights, index_ref, w_sems)
    for copy in loads + copies:
        copy.start()
    norm_pieces(loads, [place_ref[j] for j in range(len(xs))], raw, gain_ref, normed, squares)
    for copy in copies:
        copy.wait()

    @pl.loop(0, 6)
    def _(step):
        lanes = pl.ds(pl.multiple_of(step * 256, 256), 256)
        product = jnp.dot(normed[...], weights[:, lanes], preferred_element_type=jnp.float32)
        product = (product * squares[:, :1]).astype(jnp.bfloat16)
        for part, out_ref in enumerate(out_refs):
            out_ref[:, lanes] = product[part * HALF : (part + 1) * HALF]

    last = out_refs[-1]
    tail_ref[:halo, :] = last[HALF - halo :, 512:]
    tail_ref[halo:, :512] = last[HALF - 16 :, :512]
    tail_ref[halo:, 512:] = jnp.zeros((16, 512), jnp.bfloat16)


def project_in(index, places, gain, pieces, weights, moves, halo):
    any_space = pl.BlockSpec(memory_space=pl.ANY)
    vmem = pl.BlockSpec(memory_space=pltpu.VMEM)
    smem = pl.BlockSpec(memory_space=pltpu.SMEM)
    return pl.pallas_call(
        functools.partial(in_kernel, moves, len(pieces), halo),
        out_shape=[jax.ShapeDtypeStruct((HALF, 1536), jnp.bfloat16)] * 2
        + [jax.ShapeDtypeStruct((halo + 16, 1024), jnp.bfloat16)],
        in_specs=[smem, smem, vmem] + [any_space] * (len(pieces) + len(weights)),
        out_specs=[vmem] * 3,
        scratch_shapes=[
            pltpu.VMEM((8, 2 * HALF, 512), jnp.bfloat16),
            pltpu.VMEM((2 * HALF, 4096), jnp.bfloat16),
            pltpu.VMEM((4096, 1536), jnp.bfloat16),
            pltpu.VMEM((2 * HALF, LANES), jnp.float32),
            pltpu.SemaphoreType.DMA((16,)),
            pltpu.SemaphoreType.DMA((len(moves),)),
        ],
        compiler_params=pltpu.CompilerParams(vmem_limit_bytes=(44 if halo == 16 else 50) * 1024 * 1024),
        cost_estimate=pl.CostEstimate(flops=4 * HALF * 4096 * 1536, bytes_accessed=18 * 2**20, transcendentals=0),
    )(index, places, gain, *pieces, *weights)


def filter_rows(halo, taps, before_ref, main_ref, feat_ref, filter_ref, skip_ref, inner, shaped, gated, copies8):
    total = halo + HALF

    if before_ref.shape[1] == 1024:
        shaped[:16, :512] = before_ref[halo:, :512].astype(jnp.float32)
        shaped[:halo, 512:] = before_ref[:halo, :].astype(jnp.float32)
    else:
        shaped[:16, :512] = before_ref[HALF - 16 :, :512].astype(jnp.float32)
        shaped[:halo, 512:] = before_ref[HALF - halo :, 512:].astype(jnp.float32)
    shaped[16 : 16 + HALF, :512] = main_ref[:, :512].astype(jnp.float32)
    shaped[halo:total, 512:] = main_ref[:, 512:].astype(jnp.float32)

    def feature(start, size, s, lanes):
        value = None
        for j in range(3):
            tap = feat_ref[3 * j + s : 3 * j + s + 1, lanes]
            low = s * 512 + lanes.start
            term = tap * shaped[start - j : start - j + size, low : low + LANES]
            value = term if value is None else value + term
        return value

    for lane in range(0, 512, LANES):
        lanes = slice(lane, lane + LANES)
        for start in range(8, total, 64):
            size = min(64, total - start)
            gated[start : start + size, lanes] = feature(start, size, 1, lanes) * feature(start, size, 2, lanes)
        gated[:8, lanes] = jnp.zeros((8, LANES), jnp.float32)

    if taps == 7:
        for lane in range(0, 512, LANES):
            lanes = slice(lane, lane + LANES)
            for start in range(0, HALF, 64):
                own = gated[halo + start : halo + start + 64, lanes]
                value = (skip_ref[:1, lanes] + filter_ref[:1, lanes]) * own
                for j in range(1, taps):
                    value = value + filter_ref[j : j + 1, lanes] * gated[halo + start - j : halo + start - j + 64, lanes]
                inner[start : start + 64, lanes] = (feature(16 + start, 64, 0, lanes) * value).astype(jnp.bfloat16)
    else:
        for lane in range(0, 512, LANES):
            lanes = slice(lane, lane + LANES)
            for r in range(8):
                for start in range(0, HALF + 128, 128):
                    copies8[r, start : start + 128, :] = gated[16 + start - r : 16 + start - r + 128, lanes]

            @pl.loop(0, HALF // 128)
            def _(step):
                base = pl.multiple_of(step * 128, 128)
                value = jnp.zeros((128, LANES), jnp.float32)
                for r in range(8):
                    for a in range(0, 16, 4):
                        window = copies8[r, pl.ds(pl.multiple_of(base + 128 - 8 * (a + 3), 8), 128 + 24), :]
                        for b in range(4):
                            tap = filter_ref[8 * (a + b) + r : 8 * (a + b) + r + 1, lanes]
                            low = 8 * (3 - b)
                            value = value + tap * window[low : low + 128]
                copies8[8, pl.ds(base, 128), :] = value

            for start in range(0, HALF, 64):
                own = gated[halo + start : halo + start + 64, lanes]
                value = copies8[8, start : start + 64, :] + skip_ref[:1, lanes] * own
                inner[start : start + 64, lanes] = (feature(16 + start, 64, 0, lanes) * value).astype(jnp.bfloat16)


def product_rows(outs, index_ref, inner, weights, out_refs):
    z = index_ref[0]
    core = index_ref[1]
    for by in range(4):
        block = lax.rem(z + by, 4)
        if outs == 4:
            columns = pl.ds(pl.multiple_of(block * 1024, 1024), 1024)
            out_refs[by][...] = jnp.dot(
                inner[...], weights[:, columns], preferred_element_type=jnp.float32
            ).astype(jnp.bfloat16)
        else:
            for side in range(2):
                place = block * 2 + (core if side == 0 else 1 - core)
                columns = pl.ds(pl.multiple_of(place * 512, 512), 512)
                out_refs[side][by] = jnp.dot(
                    inner[...], weights[:, columns], preferred_element_type=jnp.float32
                ).astype(jnp.bfloat16)


def filter_scratch(halo, taps):
    return [
        pltpu.VMEM((halo + HALF + 16, 1536), jnp.float32),
        pltpu.VMEM((halo + HALF, 512), jnp.float32),
        pltpu.VMEM((9, 8, LANES) if taps == 7 else (9, HALF + 128, LANES), jnp.float32),
    ]


def mix_kernel(moves, halo, taps, outs, index_ref, before_ref, main_ref, feat_ref, filter_ref, skip_ref, *refs):
    count = 1 + max(m[0] for m in moves)
    ws, refs = refs[:count], refs[count:]
    out_refs, refs = refs[:outs], refs[outs:]
    shaped, gated, copies8, inner, weights, w_sems = refs
    copies = fetch(moves, ws, weights, index_ref, w_sems)
    for copy in copies:
        copy.start()
    filter_rows(halo, taps, before_ref, main_ref, feat_ref, filter_ref, skip_ref, inner, shaped, gated, copies8)
    for copy in copies:
        copy.wait()
    product_rows(outs, index_ref, inner, weights, out_refs)


def mix_out(index, before, main, feat, taps, skip, weights, moves, halo, out_shapes):
    any_space = pl.BlockSpec(memory_space=pl.ANY)
    vmem = pl.BlockSpec(memory_space=pltpu.VMEM)
    length = taps.shape[0]
    return pl.pallas_call(
        functools.partial(mix_kernel, moves, halo, length, len(out_shapes)),
        out_shape=[jax.ShapeDtypeStruct(s, jnp.bfloat16) for s in out_shapes],
        in_specs=[pl.BlockSpec(memory_space=pltpu.SMEM)] + [vmem] * 5 + [any_space] * len(weights),
        out_specs=[vmem] * len(out_shapes),
        scratch_shapes=filter_scratch(halo, length)
        + [
            pltpu.VMEM((HALF, 512), jnp.bfloat16),
            pltpu.VMEM((512, 4096), jnp.bfloat16),
            pltpu.SemaphoreType.DMA((len(moves),)),
        ],
        compiler_params=pltpu.CompilerParams(vmem_limit_bytes=48 * 1024 * 1024),
        cost_estimate=pl.CostEstimate(flops=2 * HALF * 512 * 4096, bytes_accessed=6 * 2**20, transcendentals=0),
    )(index, before, main, feat, taps, skip, *weights)


def filter_kernel(halo, taps, before_ref, main_ref, feat_ref, filter_ref, skip_ref, inner, shaped, gated, copies8):
    filter_rows(halo, taps, before_ref, main_ref, feat_ref, filter_ref, skip_ref, inner, shaped, gated, copies8)


def filtered(before, main, feat, taps, skip, halo):
    vmem = pl.BlockSpec(memory_space=pltpu.VMEM)
    length = taps.shape[0]
    return pl.pallas_call(
        functools.partial(filter_kernel, halo, length),
        out_shape=jax.ShapeDtypeStruct((HALF, 512), jnp.bfloat16),
        in_specs=[vmem] * 5,
        out_specs=vmem,
        scratch_shapes=filter_scratch(halo, length),
        compiler_params=pltpu.CompilerParams(vmem_limit_bytes=24 * 1024 * 1024),
        cost_estimate=pl.CostEstimate(flops=2 * HALF * 512 * 4096 * 3, bytes_accessed=3 * 2**20, transcendentals=0),
    )(before, main, feat, taps, skip)


def product_kernel(moves, outs, index_ref, inner, weight_ref, *refs):
    out_refs, (weights, w_sems) = refs[:outs], refs[outs:]
    copies = fetch(moves, [weight_ref], weights, index_ref, w_sems)
    for copy in copies:
        copy.start()
    for copy in copies:
        copy.wait()
    product_rows(outs, index_ref, inner, weights, out_refs)


def project_out(index, inner, weight, moves, out_shapes):
    vmem = pl.BlockSpec(memory_space=pltpu.VMEM)
    return pl.pallas_call(
        functools.partial(product_kernel, moves, len(out_shapes)),
        out_shape=[jax.ShapeDtypeStruct(s, jnp.bfloat16) for s in out_shapes],
        in_specs=[pl.BlockSpec(memory_space=pltpu.SMEM), vmem, pl.BlockSpec(memory_space=pl.ANY)],
        out_specs=[vmem] * len(out_shapes),
        scratch_shapes=[pltpu.VMEM((512, 4096), jnp.bfloat16), pltpu.SemaphoreType.DMA((len(moves),))],
        compiler_params=pltpu.CompilerParams(vmem_limit_bytes=48 * 1024 * 1024),
        cost_estimate=pl.CostEstimate(flops=2 * HALF * 512 * 4096, bytes_accessed=6 * 2**20, transcendentals=0),
    )(index, inner, weight)


def per_device(hidden, norm_gain, in_weight, feat_filter, se_filter, mr_filter, skip_gain, out_weight):
    xl, y, core, z, xh = (lax.axis_index(a) for a in AXES)
    behind = lambda place, by: (place - by) % 4
    gains = norm_gain.reshape(2, 8, 512)
    ways = (1, -1, 2)
    other_core = lambda value: shift(value, "core", 1)
    gather = lambda value, axes: by_rows(lax.all_gather(by_rows(value), axes, axis=0, tiled=False))

    side_by_side = lambda w, o: jnp.concatenate([w.reshape(256, 1536), o[:256], o[256:]], axis=1)

    whole = lax.all_gather(hidden, ("z", "xh"), axis=0, tiled=False)

    m = side_by_side(in_weight[0], out_weight[0])
    m_xl = shift(m, "xl", 1)
    m_xl, w1, o1, *m_y = together(
        m_xl, swap(in_weight[1]), swap(after(out_weight[1], m_xl)), *[shift(m, "y", by) for by in ways]
    )
    rest = shift(jnp.stack([v[:, CUT:] for v in m_y]), "xl", 1)
    most = [shift(m_xl[:, :CUT], "y", by) for by in ways]
    rest, *more = together(rest, *most, *[other_core(after(v, most[0])) for v in (m, m_xl, *m_y)])
    most, far = more[:3], more[3:]
    w_list = [m, m_xl, *m_y, *far, rest, *most] + [other_core(v) for v in (rest, *most)]
    w_moves, q_moves, slots = [], [], [z, core]

    def take(number, lead, at_xl, at_y, at_core, low, high):
        w_moves.append((number, lead, 0, min(high, 1536) - low, len(slots), low, True))
        if high == 2048:
            for half in range(2):
                q_moves.append((number, lead, 1536 + 256 * half - low, 256, len(slots), 256 * half, False))
        slots.append(at_xl * 8 + at_y * 2 + at_core)

    for number, c in ((0, core), (5, 1 - core)):
        take(number, None, xl, y, c, 0, 2048)
        take(number + 1, None, 1 - xl, y, c, 0, 2048)
        for e, by in enumerate(ways):
            take(number + 2 + e, None, xl, behind(y, by), c, 0, 2048)
    for number, c in ((10, core), (14, 1 - core)):
        for e, by in enumerate(ways):
            take(number, e, 1 - xl, behind(y, by), c, CUT, 2048)
            take(number + 1 + e, None, 1 - xl, behind(y, by), c, 0, CUT)
    q_index = jnp.stack(slots).astype(jnp.int32)
    q_list = w_list[:15]

    w1 = gather(after(w1.reshape(256, 1536), rest, *most), ("xh", "xl", "y"))
    o1 = gather(o1, ("xh", "xl", "y"))
    small = jnp.concatenate([feat_filter[1].reshape(9, 512), skip_gain[1:2], mr_filter], axis=0)

    places = jnp.arange(8, dtype=jnp.int32)
    low, high, tail = project_in(q_index, places, gains[0], [whole], w_list, w_moves, 16)
    base = other_core(lax.dynamic_index_in_dim(whole, 2 * z + 1 - core, 0, keepdims=False))
    base = jnp.where(core == xh, hidden, base)
    small = swap(after(small, low))
    tail = from_behind(tail, ("xl", "y", "core"))

    def first_parts(before, main):
        parts = mix_out(
            q_index, before, main, feat_filter[0].reshape(9, 512), se_filter, skip_gain[0:1], q_list, q_moves, 16,
            [(HALF, 1024)] * 4,
        )
        return parts[0], [shift(part, "z", by) for by, part in ((1, parts[1]), (-1, parts[3]), (2, parts[2]))]

    def over_z(own, received):
        total = own.astype(jnp.float32)
        for value in received:
            total = total + value.astype(jnp.float32)
        total = total.astype(jnp.bfloat16)
        pick = lambda c: jnp.where(c == 0, total[:, :512], total[:, 512:])
        mine, others = pick(core), pick(1 - core)
        return mine, [
            lax.ppermute(mine, ("core", "xh"), [(1, 0), (2, 3)]),
            lax.ppermute(others, ("core", "xh"), [(1, 2), (2, 1)]),
            lax.ppermute(others, ("core", "xh"), [(0, 2), (3, 1)]),
        ]

    def over_x(mine, received, rows):
        kept = jnp.where(core == xh, mine, jnp.zeros_like(mine))
        current = base[rows : rows + HALF].astype(jnp.float32) + kept.astype(jnp.float32)
        for value in received:
            current = current + value.astype(jnp.float32)
        return current.astype(jnp.bfloat16)

    own_high, high_z = first_parts(low, high)
    own_low, low_z = first_parts(tail, low)
    mine_high, high_x = over_z(own_high, high_z)
    *low_z, one, two, three = together(*low_z, *high_x)
    high = over_x(mine_high, (one, two, three), HALF)
    mine_low, low_x = over_z(own_low, low_z)
    high = after(high, low_x[2])
    high_near = [shift(high, "z", by) for by in ways]
    one, two, three, *high_near = together(*low_x, *high_near)
    low = over_x(mine_low, (one, two, three), 0)

    places = [(p, (p // 4 % 2) * 8 + (p % 4) * 2 + p // 8) for p in range(16)]
    w_moves = [(0, p, 0, 1536, None, 0, True, block) for p, block in places]
    p_moves = [(0, p, 0, 256, None, 0, False, block) for p, block in places]
    x_index = jnp.stack([behind(z, by) * 2 + c for c in (core, 1 - core) for by in (0, *ways)] * 2).astype(jnp.int32)
    low_near = [low] + [shift(low, "z", by) for by in ways]
    high_near = [high] + high_near
    high_far = [other_core(v) for v in high_near]
    low_far = [other_core(v) for v in low_near]
    p_low, p_high, tail = project_in(
        q_index, x_index, gains[1], low_near + low_far + high_near + high_far, [w1], w_moves, 144
    )
    tail = from_behind(tail, ("xl", "y", "xh"))

    def second_filter(before, main):
        return filtered(before, main, small[:9], small[10:], small[9:10], 144)

    def second_parts(inner):
        return project_out(q_index, inner, o1, p_moves, [(4, HALF, 512)] * 2)

    def second_z(own, theirs):
        both = (own.astype(jnp.float32) + theirs.astype(jnp.float32)).astype(jnp.bfloat16)
        return both[0], [shift(both[at], "z", by) for by, at in ((1, 1), (-1, 3), (2, 2))]

    def second_sum(own, received, rows):
        total = rows.astype(jnp.float32) + own.astype(jnp.float32)
        for value in received:
            total = total + value.astype(jnp.float32)
        return swap(total.astype(jnp.bfloat16))

    inner_high = second_filter(p_low, p_high)
    inner_low = second_filter(tail, p_low)
    inner_high, inner_low = together(inner_high, inner_low)
    own_high, theirs_high = second_parts(inner_high)
    theirs_high = other_core(theirs_high)
    own_high, high_z = second_z(own_high, theirs_high)
    own_low, theirs_low = second_parts(inner_low)
    theirs_low = other_core(theirs_low)
    high = second_sum(own_high, high_z, high)
    own_low, low_z = second_z(own_low, theirs_low)
    low = second_sum(own_low, low_z, low)
    return jnp.concatenate([low, high], axis=0)


def solution(mesh):
    fine = Mesh(np.asarray(mesh.devices).reshape(2, 4, 2, 4, 2), AXES)
    ctx, ch = ("xl", "y", "core"), ("z", "xh")
    return jax.shard_map(
        per_device,
        mesh=fine,
        in_specs=(
            P(ctx, ch),
            P(),
            P(None, ctx, None, ch),
            P(None, None, None, ch),
            P(None, ch),
            P(None, ch),
            P(None, ch),
            P(None, ch, ctx),
        ),
        out_specs=P(ctx, ch),
        check_vma=False,
    )
```

profile of v0, /device:TPU:3, one launch (start us, length us, event | category | flops | bytes accessed | tf_op | source)
XLA Modules:
  0.0 332.3 jit_solution(7355808890473065951)
XLA Ops:
  11.3 5.1 %collective-permute-start.2 = (bf16[256,3,512]{0,2,1:T(8,128)(2,1)}, bf16[256,3,512]{0,2,1:T(8,128)(2,1)}, u32[]{:S(2)}, u32[]{:S(2)}) collective-permute-start(bf16[256,3,512]{0,2,1:T(8,128)(2,1)} %bitcast.23), channel_id=1, source_target_pairs={{1,8},{8,1},{3,10},{10,3},{5,12},{12,5},{7,14},{14,7},{17,24},{24,... | collective-permute-start | bytes 2359304 | tf_op jit(solution)/shard_map/ppermute | solution.py:24
  21.8 17.9 %collective-permute-done.1.refs_2_.refs_1_ = bf16[256,2048]{1,0:T(8,128)(2,1)S(1)} collective-permute-done((bf16[256,2048]{1,0:T(8,128)(2,1)S(1)}, bf16[256,2048]{1,0:T(8,128)(2,1)S(1)}, u32[]{:S(2)}, u32[]{:S(2)}) %collective-permute-start.1) | collective-permute-done | bytes 1048608 | tf_op jit(solution)/shard_map/ppermute | solution.py:20
  39.7 5.2 %collective-permute-start.3 = (bf16[512,256]{1,0:T(8,128)(2,1)S(1)}, bf16[512,256]{1,0:T(8,128)(2,1)S(1)}, u32[]{:S(2)}, u32[]{:S(2)}) collective-permute-start(bf16[512,256]{1,0:T(8,128)(2,1)S(1)} %slice_bitcast_fusion.11), channel_id=1, source_target_pairs={{1,8},{8,1},{3,10},{10,3},{5,12},{12,5},{7,14},{14,7},{17,24},{24,... | collective-permute-start | bytes 786440 | tf_op jit(solution)/shard_map/ppermute | solution.py:24
  44.9 5.4 %collective-permute-done.2 = bf16[256,3,512]{0,2,1:T(8,128)(2,1)} collective-permute-done((bf16[256,3,512]{0,2,1:T(8,128)(2,1)}, bf16[256,3,512]{0,2,1:T(8,128)(2,1)}, u32[]{:S(2)}, u32[]{:S(2)}) %collective-permute-start.2) | collective-permute-done | bytes 786464 | tf_op jit(solution)/shard_map/ppermute | solution.py:24
  50.3 2.3 broadcast_select_fusion
  53.9 10.5 %collective-permute-done.6.refs_5_.refs_4_ = bf16[256,2048]{1,0:T(8,128)(2,1)} collective-permute-done((bf16[256,2048]{1,0:T(8,128)(2,1)S(1)}, bf16[256,2048]{1,0:T(8,128)(2,1)}, u32[]{:S(2)}, u32[]{:S(2)}) %collective-permute-start.6) | collective-permute-done | bytes 1048608 | tf_op jit(solution)/shard_map/ppermute | solution.py:20
  70.5 14.4 %collective-permute-done.8.refs_12_.refs_11_ = bf16[256,1280]{1,0:T(8,128)(2,1)S(1)} collective-permute-done((bf16[256,1280]{1,0:T(8,128)(2,1)S(1)}, bf16[256,1280]{1,0:T(8,128)(2,1)S(1)}, u32[]{:S(2)}, u32[]{:S(2)}) %collective-permute-start.8) | collective-permute-done | bytes 655392 | tf_op jit(solution)/shard_map/ppermute | solution.py:20
  85.5 12.8 %collective-permute-done.10.refs_14_.refs_13_ = bf16[256,1280]{1,0:T(8,128)(2,1)S(1)} collective-permute-done((bf16[256,1280]{1,0:T(8,128)(2,1)S(1)}, bf16[256,1280]{1,0:T(8,128)(2,1)S(1)}, u32[]{:S(2)}, u32[]{:S(2)}) %collective-permute-start.10) | collective-permute-done | bytes 655392 | tf_op jit(solution)/shard_map/ppermute | solution.py:20
  98.4 3.4 %collective-permute-done.7.refs_11_.refs_10_ = bf16[3,256,768]{2,1,0:T(8,128)(2,1)S(1)} collective-permute-done((bf16[3,256,768]{2,1,0:T(8,128)(2,1)S(1)}, bf16[3,256,768]{2,1,0:T(8,128)(2,1)S(1)}, u32[]{:S(2)}, u32[]{:S(2)}) %collective-permute-start.7) | collective-permute-done | bytes 1179680 | tf_op jit(solution)/shard_map/ppermute | solution.py:20
  102.2 2.4 collective-permute-done.15.refs_10_.refs_9_
  105.7 2.3 copy.14
  118.2 14.0 %shard_map.82 = (bf16[256,1536]{1,0:T(8,128)(2,1)S(1)}, bf16[256,1536]{1,0:T(8,128)(2,1)S(1)}, bf16[32,1024]{1,0:T(8,128)(2,1)S(1)}) custom-call(s32[24]{0:T(128)S(1)} %stack.128.index_ref, s32[8]{0:T(128)S(1)} %iota.3.place_ref, f32[8,512]{1,0:T(8,128)S(1)} %squeeze.38.gain_ref, bf16[8,512,512]{2,1,0:T(8,128)(2,1)} %bitcast.73, ...), custom_call_target="tpu_custom_call" | custom-call | flops 6442450944 | bytes 18874368 | tf_op jit(solution)/shard_map/pallas_call | solution.py:118
  133.5 5.5 %shard_map.84 = (bf16[256,1024]{1,0:T(8,128)(2,1)S(1)}, bf16[256,1024]{1,0:T(8,128)(2,1)}, bf16[256,1024]{1,0:T(8,128)(2,1)}, bf16[256,1024]{1,0:T(8,128)(2,1)}) custom-call(s32[24]{0:T(128)S(1)} %copy-done.24, bf16[256,1536]{1,0:T(8,128)(2,1)S(1)} %get-tuple-element.81.main_ref.before_ref, bf16[256,1536]{1,0:T(8,128)(2,1)S(1)} %get-tuple-element.86.main_ref, ...), custom_call_target="tpu_custom_call" | custom-call | flops 1073741824 | bytes 6291456 | tf_op jit(solution)/shard_map/pallas_call | solution.py:245
  139.0 3.1 collective-permute-start.26
  143.7 4.2 %collective-permute-start.20 = (bf16[32,1024]{1,0:T(8,128)(2,1)}, bf16[32,1024]{1,0:T(8,128)(2,1)S(1)}, u32[]{:S(2)}, u32[]{:S(2)}) collective-permute-start(bf16[32,1024]{1,0:T(8,128)(2,1)} %copy-done.27), channel_id=1, source_target_pairs={{0,8},{8,16},{16,24},{24,32},{32,40},{40,48},{48,56},{56,64},{64,7... | collective-permute-start | bytes 196616 | tf_op jit(solution)/shard_map/ppermute | solution.py:30
  154.0 4.5 %shard_map.83 = (bf16[256,1024]{1,0:T(8,128)(2,1)S(1)}, bf16[256,1024]{1,0:T(8,128)(2,1)S(1)}, bf16[256,1024]{1,0:T(8,128)(2,1)S(1)}, bf16[256,1024]{1,0:T(8,128)(2,1)S(1)}) custom-call(s32[24]{0:T(128)S(1)} %copy-done.25, bf16[32,1024]{1,0:T(8,128)(2,1)S(1)} %collective-permute-done.20.before_ref, bf16[256,1536]{1,0:T(8,128)(2,1)S(1)} %copy-done.5, ...), custom_call_target="tpu_custom_call" | custom-call | flops 1073741824 | bytes 6291456 | tf_op jit(solution)/shard_map/pallas_call | solution.py:245
  158.7 2.6 collective-permute-start.22
  161.3 4.6 %collective-permute-done.25 = bf16[256,1024]{1,0:T(8,128)(2,1)} collective-permute-done((bf16[256,1024]{1,0:T(8,128)(2,1)}, bf16[256,1024]{1,0:T(8,128)(2,1)}, u32[]{:S(2)}, u32[]{:S(2)}) %collective-permute-start.25) | collective-permute-done | bytes 524320 | tf_op jit(solution)/shard_map/ppermute | solution.py:20
  167.4 1.8 add_convert_fusion.3
  169.3 6.4 %collective-permute-start.28 = (bf16[256,512]{1,0:T(8,128)(2,1)S(1)}, bf16[256,512]{1,0:T(8,128)(2,1)S(1)}, u32[]{:S(2)}, u32[]{:S(2)}) collective-permute-start(bf16[256,512]{1,0:T(8,128)(2,1)S(1)} %get-tuple-element.131), channel_id=1, source_target_pairs={{1,8},{8,1},{3,10},{10,3},{5,12},{12,5},{7,14},{14,7},{17,24},{24,... | collective-permute-start | bytes 786440 | tf_op jit(solution)/shard_map/ppermute | solution.py:372
  177.9 4.3 %collective-permute-start.27 = (bf16[256,512]{1,0:T(8,128)(2,1)S(1)}, bf16[256,512]{1,0:T(8,128)(2,1)S(1)}, u32[]{:S(2)}, u32[]{:S(2)}) collective-permute-start(bf16[256,512]{1,0:T(8,128)(2,1)S(1)} %get-tuple-element.132), channel_id=1, source_target_pairs={{1,0},{8,9},{3,2},{10,11},{5,4},{12,13},{7,6},{14,15},{17,16},{24,... | collective-permute-start | bytes 786440 | tf_op jit(solution)/shard_map/ppermute | solution.py:371
  182.3 5.6 %collective-permute-done.23 = bf16[256,1024]{1,0:T(8,128)(2,1)S(1)} collective-permute-done((bf16[256,1024]{1,0:T(8,128)(2,1)S(1)}, bf16[256,1024]{1,0:T(8,128)(2,1)S(1)}, u32[]{:S(2)}, u32[]{:S(2)}) %collective-permute-start.23) | collective-permute-done | bytes 524320 | tf_op jit(solution)/shard_map/ppermute | solution.py:20
  187.9 5.0 %collective-permute-done.27 = bf16[256,512]{1,0:T(8,128)(2,1)S(1)} collective-permute-done((bf16[256,512]{1,0:T(8,128)(2,1)S(1)}, bf16[256,512]{1,0:T(8,128)(2,1)S(1)}, u32[]{:S(2)}, u32[]{:S(2)}) %collective-permute-start.27) | collective-permute-done | bytes 262176 | tf_op jit(solution)/shard_map/ppermute | solution.py:371
  193.4 2.5 collective-permute-start.31
  197.2 5.3 %collective-permute-start.30 = (bf16[256,512]{1,0:T(8,128)(2,1)S(1)}, bf16[256,512]{1,0:T(8,128)(2,1)S(1)}, u32[]{:S(2)}, u32[]{:S(2)}) collective-permute-start(bf16[256,512]{1,0:T(8,128)(2,1)S(1)} %get-tuple-element.130), channel_id=1, source_target_pairs={{1,0},{8,9},{3,2},{10,11},{5,4},{12,13},{7,6},{14,15},{17,16},{24,... | collective-permute-start | bytes 786440 | tf_op jit(solution)/shard_map/ppermute | solution.py:371
  206.2 1.8 collective-permute-done.30
  208.0 3.1 collective-permute-start.43
  211.1 4.1 %collective-permute-done.33.refs_9_ = bf16[256,512]{1,0:T(8,128)(2,1)S(1)} collective-permute-done((bf16[256,512]{1,0:T(8,128)(2,1)S(1)}, bf16[256,512]{1,0:T(8,128)(2,1)S(1)}, u32[]{:S(2)}, u32[]{:S(2)}) %collective-permute-start.33) | collective-permute-done | bytes 262176 | tf_op jit(solution)/shard_map/ppermute | solution.py:20
  216.7 1.9 collective-permute-start.37
  220.2 4.5 %collective-permute-done.36.refs_1_ = bf16[256,512]{1,0:T(8,128)(2,1)S(1)} collective-permute-done((bf16[256,512]{1,0:T(8,128)(2,1)S(1)}, bf16[256,512]{1,0:T(8,128)(2,1)S(1)}, u32[]{:S(2)}, u32[]{:S(2)}) %collective-permute-start.36) | collective-permute-done | bytes 262176 | tf_op jit(solution)/shard_map/ppermute | solution.py:20
  224.7 4.8 %collective-permute-done.37.refs_2_ = bf16[256,512]{1,0:T(8,128)(2,1)S(1)} collective-permute-done((bf16[256,512]{1,0:T(8,128)(2,1)S(1)}, bf16[256,512]{1,0:T(8,128)(2,1)S(1)}, u32[]{:S(2)}, u32[]{:S(2)}) %collective-permute-start.37) | collective-permute-done | bytes 262176 | tf_op jit(solution)/shard_map/ppermute | solution.py:20
  231.3 1.7 pad_maximum_fusion.3
  233.0 2.9 collective-permute-start.47
  235.9 14.6 %shard_map.85 = (bf16[256,1536]{1,0:T(8,128)(2,1)}, bf16[256,1536]{1,0:T(8,128)(2,1)}, bf16[160,1024]{1,0:T(8,128)(2,1)}) custom-call(s32[24]{0:T(128)S(1)} %copy-done.26, s32[16]{0:T(128)S(1)} %stack.141.place_ref, f32[8,512]{1,0:T(8,128)S(1)} %squeeze.41.gain_ref, bf16[256,512]{1,0:T(8,128)(2,1)S(1)} %add_convert_fusion.4.refs_0_, ...), custom_call_target="tpu_custom_call" | custom-call | flops 6442450944 | bytes 18874368 | tf_op jit(solution)/shard_map/pallas_call | solution.py:118
  250.6 2.2 collective-permute-start.48
  256.1 8.7 %shard_map.86.inner = bf16[256,512]{1,0:T(8,128)(2,1)S(1)} custom-call(bf16[256,1536]{1,0:T(8,128)(2,1)S(1)} %copy-done.28, bf16[256,1536]{1,0:T(8,128)(2,1)S(1)} %copy-done.29, f32[9,512]{1,0:T(8,128)S(1)} %slice.158.feat_ref, f32[128,512]{1,0:T(8,128)S(1)} %slice.159.filter_ref, f32[1,512]{1,0:T(1,128)S(1)} %slice.160.skip_ref), custom_call_target="tpu_custom_call" | custom-call | flops 3221225472 | bytes 3145728 | tf_op jit(solution)/shard_map/pallas_call | solution.py:268
  264.9 5.1 %collective-permute-done.48.before_ref = bf16[160,1024]{1,0:T(8,128)(2,1)S(1)} collective-permute-done((bf16[160,1024]{1,0:T(8,128)(2,1)}, bf16[160,1024]{1,0:T(8,128)(2,1)S(1)}, u32[]{:S(2)}, u32[]{:S(2)}) %collective-permute-start.48) | collective-permute-done | bytes 327712 | tf_op jit(solution)/shard_map/ppermute | solution.py:30
  270.0 8.7 %shard_map.87.inner = bf16[256,512]{1,0:T(8,128)(2,1)S(1)} custom-call(bf16[160,1024]{1,0:T(8,128)(2,1)S(1)} %collective-permute-done.48.before_ref, bf16[256,1536]{1,0:T(8,128)(2,1)S(1)} %copy-done.28, f32[9,512]{1,0:T(8,128)S(1)} %slice.158.feat_ref, f32[128,512]{1,0:T(8,128)S(1)} %slice.159.filter_ref, f32[1,512]{1,0:T(1,128)S(1)} %slice.160.skip_ref), custom_call_target="tpu_custom_call" | custom-call | flops 3221225472 | bytes 3145728 | tf_op jit(solution)/shard_map/pallas_call | solution.py:268
  278.8 4.1 %shard_map.89 = (bf16[4,256,512]{2,1,0:T(8,128)(2,1)S(1)}, bf16[4,256,512]{2,1,0:T(8,128)(2,1)S(1)}) custom-call(s32[24]{0:T(128)S(1)} %copy-done.26, bf16[256,512]{1,0:T(8,128)(2,1)S(1)} %shard_map.86.inner, bf16[16,512,256]{2,1,0:T(8,128)(2,1)} %bitcast.69), custom_call_target="tpu_custom_call" | custom-call | flops 1073741824 | bytes 6291456 | tf_op jit(solution)/shard_map/pallas_call | solution.py:291
  283.5 4.1 %shard_map.88 = (bf16[4,256,512]{2,1,0:T(8,128)(2,1)S(1)}, bf16[4,256,512]{2,1,0:T(8,128)(2,1)S(1)}) custom-call(s32[24]{0:T(128)S(1)} %copy-done.26, bf16[256,512]{1,0:T(8,128)(2,1)S(1)} %shard_map.87.inner, bf16[16,512,256]{2,1,0:T(8,128)(2,1)} %bitcast.70), custom_call_target="tpu_custom_call" | custom-call | flops 1073741824 | bytes 6291456 | tf_op jit(solution)/shard_map/pallas_call | solution.py:291
  288.3 2.0 collective-permute-start.57
  290.3 1.7 collective-permute-start.56
  293.9 2.1 collective-permute-start.51
  298.6 4.7 %collective-permute-done.56 = bf16[256,512]{1,0:T(8,128)(2,1)S(1)} collective-permute-done((bf16[256,512]{1,0:T(8,128)(2,1)S(1)}, bf16[256,512]{1,0:T(8,128)(2,1)S(1)}, u32[]{:S(2)}, u32[]{:S(2)}) %collective-permute-start.56) | collective-permute-done | bytes 262176 | tf_op jit(solution)/shard_map/ppermute | solution.py:20
  304.8 2.3 collective-permute-start.58
  308.6 5.9 %collective-permute-done.51 = bf16[256,512]{1,0:T(8,128)(2,1)S(1)} collective-permute-done((bf16[256,512]{1,0:T(8,128)(2,1)S(1)}, bf16[256,512]{1,0:T(8,128)(2,1)S(1)}, u32[]{:S(2)}, u32[]{:S(2)}) %collective-permute-start.51) | collective-permute-done | bytes 262176 | tf_op jit(solution)/shard_map/ppermute | solution.py:20
  315.2 2.3 collective-permute-start.53
  317.5 6.9 %collective-permute-done.53 = bf16[256,512]{1,0:T(8,128)(2,1)S(1)} collective-permute-done((bf16[256,512]{1,0:T(8,128)(2,1)S(1)}, bf16[256,512]{1,0:T(8,128)(2,1)S(1)}, u32[]{:S(2)}, u32[]{:S(2)}) %collective-permute-start.53) | collective-permute-done | bytes 262176 | tf_op jit(solution)/shard_map/ppermute | solution.py:24
  (221 shorter events, 66.3 us)
Async XLA Ops:
  6.5 108.3 %all-gather.7.cloned.1.call-start = ((), (), s32[]{:S(2)}) async-start(), calls=%async_computation | async-start | bytes 4718592 | tf_op jit(solution)/shard_map/all_gather | solution.py:312
  7.3 228.7 %all-gather.9.cloned.1.call-start = ((), (), s32[]{:S(2)}) async-start(), calls=%async_computation.1 | async-start | bytes 13369344 | tf_op jit(solution)/shard_map/all_gather | solution.py:308
  10.0 29.7 %collective-permute-start.1 = (bf16[256,2048]{1,0:T(8,128)(2,1)S(1)}, bf16[256,2048]{1,0:T(8,128)(2,1)S(1)}, u32[]{:S(2)}, u32[]{:S(2)}) collective-permute-start(bf16[256,2048]{1,0:T(8,128)(2,1)S(1)} %pad_maximum_fusion.1.refs_1_.refs_0_), channel_id=1, source_target_pairs={{0,64},{64,0},{1,65},{65,1},{2,66},{66,2},{3,67},{67,3},{4,68},{68... | collective-permute-start | bytes 3145736 | tf_op jit(solution)/shard_map/ppermute | solution.py:20
  11.3 39.1 %collective-permute-start.2 = (bf16[256,3,512]{0,2,1:T(8,128)(2,1)}, bf16[256,3,512]{0,2,1:T(8,128)(2,1)}, u32[]{:S(2)}, u32[]{:S(2)}) collective-permute-start(bf16[256,3,512]{0,2,1:T(8,128)(2,1)} %bitcast.23), channel_id=1, source_target_pairs={{1,8},{8,1},{3,10},{10,3},{5,12},{12,5},{7,14},{14,7},{17,24},{24,... | collective-permute-start | bytes 2359304 | tf_op jit(solution)/shard_map/ppermute | solution.py:24
  16.4 37.5 %collective-permute-start.4 = (bf16[256,2048]{1,0:T(8,128)(2,1)S(1)}, bf16[256,2048]{1,0:T(8,128)(2,1)S(1)}, u32[]{:S(2)}, u32[]{:S(2)}) collective-permute-start(bf16[256,2048]{1,0:T(8,128)(2,1)S(1)} %pad_maximum_fusion.1.refs_1_.refs_0_), channel_id=1, source_target_pairs={{0,16},{16,32},{32,48},{48,0},{1,17},{17,33},{33,49},{49,1},{2,18}... | collective-permute-start | bytes 3145736 | tf_op jit(solution)/shard_map/ppermute | solution.py:20
  17.7 36.1 %collective-permute-start.5 = (bf16[256,2048]{1,0:T(8,128)(2,1)S(1)}, bf16[256,2048]{1,0:T(8,128)(2,1)}, u32[]{:S(2)}, u32[]{:S(2)}) collective-permute-start(bf16[256,2048]{1,0:T(8,128)(2,1)S(1)} %pad_maximum_fusion.1.refs_1_.refs_0_), channel_id=1, source_target_pairs={{0,48},{16,0},{32,16},{48,32},{1,49},{17,1},{33,17},{49,33},{2,50}... | collective-permute-start | bytes 3145736 | tf_op jit(solution)/shard_map/ppermute | solution.py:20
  19.3 45.1 %collective-permute-start.6 = (bf16[256,2048]{1,0:T(8,128)(2,1)S(1)}, bf16[256,2048]{1,0:T(8,128)(2,1)}, u32[]{:S(2)}, u32[]{:S(2)}) collective-permute-start(bf16[256,2048]{1,0:T(8,128)(2,1)S(1)} %pad_maximum_fusion.1.refs_1_.refs_0_), channel_id=1, source_target_pairs={{0,32},{16,48},{32,0},{48,16},{1,33},{17,49},{33,1},{49,17},{2,34}... | collective-permute-start | bytes 3145736 | tf_op jit(solution)/shard_map/ppermute | solution.py:20
  39.7 13.4 %collective-permute-start.3 = (bf16[512,256]{1,0:T(8,128)(2,1)S(1)}, bf16[512,256]{1,0:T(8,128)(2,1)S(1)}, u32[]{:S(2)}, u32[]{:S(2)}) collective-permute-start(bf16[512,256]{1,0:T(8,128)(2,1)S(1)} %slice_bitcast_fusion.11), channel_id=1, source_target_pairs={{1,8},{8,1},{3,10},{10,3},{5,12},{12,5},{7,14},{14,7},{17,24},{24,... | collective-permute-start | bytes 786440 | tf_op jit(solution)/shard_map/ppermute | solution.py:24
  65.8 36.0 %collective-permute-start.7 = (bf16[3,256,768]{2,1,0:T(8,128)(2,1)S(1)}, bf16[3,256,768]{2,1,0:T(8,128)(2,1)S(1)}, u32[]{:S(2)}, u32[]{:S(2)}) collective-permute-start(bf16[3,256,768]{2,1,0:T(8,128)(2,1)S(1)} %pad_maximum_fusion), channel_id=1, source_target_pairs={{0,64},{64,0},{1,65},{65,1},{2,66},{66,2},{3,67},{67,3},{4,68},{68... | collective-permute-start | bytes 3538952 | tf_op jit(solution)/shard_map/ppermute | solution.py:20
  67.4 17.5 %collective-permute-start.8 = (bf16[256,1280]{1,0:T(8,128)(2,1)S(1)}, bf16[256,1280]{1,0:T(8,128)(2,1)S(1)}, u32[]{:S(2)}, u32[]{:S(2)}) collective-permute-start(bf16[256,1280]{1,0:T(8,128)(2,1)S(1)} %slice.130), channel_id=1, source_target_pairs={{0,16},{16,32},{32,48},{48,0},{1,17},{17,33},{33,49},{49,1},{2,18}... | collective-permute-start | bytes 1966088 | tf_op jit(solution)/shard_map/ppermute | solution.py:20
  68.6 16.8 %collective-permute-start.9 = (bf16[256,1280]{1,0:T(8,128)(2,1)S(1)}, bf16[256,1280]{1,0:T(8,128)(2,1)S(1)}, u32[]{:S(2)}, u32[]{:S(2)}) collective-permute-start(bf16[256,1280]{1,0:T(8,128)(2,1)S(1)} %slice.130), channel_id=1, source_target_pairs={{0,48},{16,0},{32,16},{48,32},{1,49},{17,1},{33,17},{49,33},{2,50}... | collective-permute-start | bytes 1966088 | tf_op jit(solution)/shard_map/ppermute | solution.py:20
  70.2 28.2 %collective-permute-start.10 = (bf16[256,1280]{1,0:T(8,128)(2,1)S(1)}, bf16[256,1280]{1,0:T(8,128)(2,1)S(1)}, u32[]{:S(2)}, u32[]{:S(2)}) collective-permute-start(bf16[256,1280]{1,0:T(8,128)(2,1)S(1)} %slice.130), channel_id=1, source_target_pairs={{0,32},{16,48},{32,0},{48,16},{1,33},{17,49},{33,1},{49,17},{2,34}... | collective-permute-start | bytes 1966088 | tf_op jit(solution)/shard_map/ppermute | solution.py:20
  84.9 17.2 %collective-permute-start.11 = (bf16[256,2048]{1,0:T(8,128)(2,1)S(1)}, bf16[256,2048]{1,0:T(8,128)(2,1)S(1)}, u32[]{:S(2)}, u32[]{:S(2)}) collective-permute-start(bf16[256,2048]{1,0:T(8,128)(2,1)S(1)} %pad_maximum_fusion.1.refs_1_.refs_0_), channel_id=1, source_target_pairs={{0,8},{8,0},{1,9},{9,1},{2,10},{10,2},{3,11},{11,3},{4,12},{12,4},... | collective-permute-start | bytes 3145736 | tf_op jit(solution)/shard_map/ppermute | solution.py:20
  84.9 17.2 %collective-permute-start.12 = (bf16[256,2048]{1,0:T(8,128)(2,1)S(1)}, bf16[256,2048]{1,0:T(8,128)(2,1)S(1)}, u32[]{:S(2)}, u32[]{:S(2)}) collective-permute-start(bf16[256,2048]{1,0:T(8,128)(2,1)S(1)} %collective-permute-done.1.refs_2_.refs_1_), channel_id=1, source_target_pairs={{0,8},{8,0},{1,9},{9,1},{2,10},{10,2},{3,11},{11,3},{4,12},{12,4},... | collective-permute-start | bytes 3145736 | tf_op jit(solution)/shard_map/ppermute | solution.py:20
  85.5 16.7 %collective-permute-start.13 = (bf16[256,2048]{1,0:T(8,128)(2,1)S(1)}, bf16[256,2048]{1,0:T(8,128)(2,1)S(1)}, u32[]{:S(2)}, u32[]{:S(2)}) collective-permute-start(bf16[256,2048]{1,0:T(8,128)(2,1)S(1)} %collective-permute-done.4.refs_3_.refs_2_), channel_id=1, source_target_pairs={{0,8},{8,0},{1,9},{9,1},{2,10},{10,2},{3,11},{11,3},{4,12},{12,4},... | collective-permute-start | bytes 3145736 | tf_op jit(solution)/shard_map/ppermute | solution.py:20
  108.0 170.8 %all-gather.11.cloned.1.call-start = ((), (), s32[]{:S(2)}) async-start(), calls=%async_computation.2 | async-start | bytes 4456448 | tf_op jit(solution)/shard_map/all_gather | solution.py:308
  139.0 19.6 %collective-permute-start.26 = (bf16[256,1024]{1,0:T(8,128)(2,1)}, bf16[256,1024]{1,0:T(8,128)(2,1)}, u32[]{:S(2)}, u32[]{:S(2)}) collective-permute-start(bf16[256,1024]{1,0:T(8,128)(2,1)} %get-tuple-element.90), channel_id=1, source_target_pairs={{0,4},{2,6},{4,0},{6,2},{1,5},{3,7},{5,1},{7,3},{8,12},{10,14},{12... | collective-permute-start | bytes 1572872 | tf_op jit(solution)/shard_map/ppermute | solution.py:20
  142.2 23.6 %collective-permute-start.25 = (bf16[256,1024]{1,0:T(8,128)(2,1)}, bf16[256,1024]{1,0:T(8,128)(2,1)}, u32[]{:S(2)}, u32[]{:S(2)}) collective-permute-start(bf16[256,1024]{1,0:T(8,128)(2,1)} %get-tuple-element.89), channel_id=1, source_target_pairs={{0,6},{2,0},{4,2},{6,4},{1,7},{3,1},{5,3},{7,5},{8,14},{10,8},{12,... | collective-permute-start | bytes 1572872 | tf_op jit(solution)/shard_map/ppermute | solution.py:20
  143.0 24.4 %collective-permute-start.24 = (bf16[256,1024]{1,0:T(8,128)(2,1)}, bf16[256,1024]{1,0:T(8,128)(2,1)}, u32[]{:S(2)}, u32[]{:S(2)}) collective-permute-start(bf16[256,1024]{1,0:T(8,128)(2,1)} %get-tuple-element.88), channel_id=1, source_target_pairs={{0,2},{2,4},{4,6},{6,0},{1,3},{3,5},{5,7},{7,1},{8,10},{10,12},{12... | collective-permute-start | bytes 1572872 | tf_op jit(solution)/shard_map/ppermute | solution.py:20
  148.9 26.7 %collective-permute-start = (bf16[512,512]{1,0:T(8,128)(2,1)S(1)}, bf16[512,512]{1,0:T(8,128)(2,1)S(1)}, u32[]{:S(2)}, u32[]{:S(2)}) collective-permute-start(bf16[512,512]{1,0:T(8,128)(2,1)S(1)} %dynamic-slice_bitcast_fusion), channel_id=1, source_target_pairs={{0,8},{8,0},{1,9},{9,1},{2,10},{10,2},{3,11},{11,3},{4,12},{12,4},... | collective-permute-start | bytes 1572872 | tf_op jit(solution)/shard_map/ppermute | solution.py:20
  158.5 19.4 %collective-permute-start.21 = (bf16[256,1024]{1,0:T(8,128)(2,1)S(1)}, bf16[256,1024]{1,0:T(8,128)(2,1)S(1)}, u32[]{:S(2)}, u32[]{:S(2)}) collective-permute-start(bf16[256,1024]{1,0:T(8,128)(2,1)S(1)} %get-tuple-element.83), channel_id=1, source_target_pairs={{0,2},{2,4},{4,6},{6,0},{1,3},{3,5},{5,7},{7,1},{8,10},{10,12},{12... | collective-permute-start | bytes 1572872 | tf_op jit(solution)/shard_map/ppermute | solution.py:20
  158.7 23.6 %collective-permute-start.22 = (bf16[256,1024]{1,0:T(8,128)(2,1)S(1)}, bf16[256,1024]{1,0:T(8,128)(2,1)S(1)}, u32[]{:S(2)}, u32[]{:S(2)}) collective-permute-start(bf16[256,1024]{1,0:T(8,128)(2,1)S(1)} %get-tuple-element.84), channel_id=1, source_target_pairs={{0,6},{2,0},{4,2},{6,4},{1,7},{3,1},{5,3},{7,5},{8,14},{10,8},{12,... | collective-permute-start | bytes 1572872 | tf_op jit(solution)/shard_map/ppermute | solution.py:20
  165.8 22.1 %collective-permute-start.23 = (bf16[256,1024]{1,0:T(8,128)(2,1)S(1)}, bf16[256,1024]{1,0:T(8,128)(2,1)S(1)}, u32[]{:S(2)}, u32[]{:S(2)}) collective-permute-start(bf16[256,1024]{1,0:T(8,128)(2,1)S(1)} %get-tuple-element.85), channel_id=1, source_target_pairs={{0,4},{2,6},{4,0},{6,2},{1,5},{3,7},{5,1},{7,3},{8,12},{10,14},{12... | collective-permute-start | bytes 1572872 | tf_op jit(solution)/shard_map/ppermute | solution.py:20
  169.3 23.7 %collective-permute-start.28 = (bf16[256,512]{1,0:T(8,128)(2,1)S(1)}, bf16[256,512]{1,0:T(8,128)(2,1)S(1)}, u32[]{:S(2)}, u32[]{:S(2)}) collective-permute-start(bf16[256,512]{1,0:T(8,128)(2,1)S(1)} %get-tuple-element.131), channel_id=1, source_target_pairs={{1,8},{8,1},{3,10},{10,3},{5,12},{12,5},{7,14},{14,7},{17,24},{24,... | collective-permute-start | bytes 786440 | tf_op jit(solution)/shard_map/ppermute | solution.py:372
  175.7 17.3 %collective-permute-start.29 = (bf16[256,512]{1,0:T(8,128)(2,1)S(1)}, bf16[256,512]{1,0:T(8,128)(2,1)S(1)}, u32[]{:S(2)}, u32[]{:S(2)}) collective-permute-start(bf16[256,512]{1,0:T(8,128)(2,1)S(1)} %get-tuple-element.131), channel_id=1, source_target_pairs={{0,8},{9,1},{2,10},{11,3},{4,12},{13,5},{6,14},{15,7},{16,24},{25,... | collective-permute-start | bytes 786440 | tf_op jit(solution)/shard_map/ppermute | solution.py:373
  177.9 15.0 %collective-permute-start.27 = (bf16[256,512]{1,0:T(8,128)(2,1)S(1)}, bf16[256,512]{1,0:T(8,128)(2,1)S(1)}, u32[]{:S(2)}, u32[]{:S(2)}) collective-permute-start(bf16[256,512]{1,0:T(8,128)(2,1)S(1)} %get-tuple-element.132), channel_id=1, source_target_pairs={{1,0},{8,9},{3,2},{10,11},{5,4},{12,13},{7,6},{14,15},{17,16},{24,... | collective-permute-start | bytes 786440 | tf_op jit(solution)/shard_map/ppermute | solution.py:371
  193.4 17.7 %collective-permute-start.31 = (bf16[256,512]{1,0:T(8,128)(2,1)S(1)}, bf16[256,512]{1,0:T(8,128)(2,1)S(1)}, u32[]{:S(2)}, u32[]{:S(2)}) collective-permute-start(bf16[256,512]{1,0:T(8,128)(2,1)S(1)} %get-tuple-element.129), channel_id=1, source_target_pairs={{1,8},{8,1},{3,10},{10,3},{5,12},{12,5},{7,14},{14,7},{17,24},{24,... | collective-permute-start | bytes 786440 | tf_op jit(solution)/shard_map/ppermute | solution.py:372
  197.2 10.8 %collective-permute-start.30 = (bf16[256,512]{1,0:T(8,128)(2,1)S(1)}, bf16[256,512]{1,0:T(8,128)(2,1)S(1)}, u32[]{:S(2)}, u32[]{:S(2)}) collective-permute-start(bf16[256,512]{1,0:T(8,128)(2,1)S(1)} %get-tuple-element.130), channel_id=1, source_target_pairs={{1,0},{8,9},{3,2},{10,11},{5,4},{12,13},{7,6},{14,15},{17,16},{24,... | collective-permute-start | bytes 786440 | tf_op jit(solution)/shard_map/ppermute | solution.py:371
  202.8 12.5 %collective-permute-start.33 = (bf16[256,512]{1,0:T(8,128)(2,1)S(1)}, bf16[256,512]{1,0:T(8,128)(2,1)S(1)}, u32[]{:S(2)}, u32[]{:S(2)}) collective-permute-start(bf16[256,512]{1,0:T(8,128)(2,1)S(1)} %add_convert_fusion.5.refs_8_), channel_id=1, source_target_pairs={{0,2},{2,4},{4,6},{6,0},{1,3},{3,5},{5,7},{7,1},{8,10},{10,12},{12... | collective-permute-start | bytes 786440 | tf_op jit(solution)/shard_map/ppermute | solution.py:20
  204.0 11.3 %collective-permute-start.34 = (bf16[256,512]{1,0:T(8,128)(2,1)S(1)}, bf16[256,512]{1,0:T(8,128)(2,1)S(1)}, u32[]{:S(2)}, u32[]{:S(2)}) collective-permute-start(bf16[256,512]{1,0:T(8,128)(2,1)S(1)} %add_convert_fusion.5.refs_8_), channel_id=1, source_target_pairs={{0,6},{2,0},{4,2},{6,4},{1,7},{3,1},{5,3},{7,5},{8,14},{10,8},{12,... | collective-permute-start | bytes 786440 | tf_op jit(solution)/shard_map/ppermute | solution.py:20
  205.5 9.8 %collective-permute-start.35 = (bf16[256,512]{1,0:T(8,128)(2,1)S(1)}, bf16[256,512]{1,0:T(8,128)(2,1)S(1)}, u32[]{:S(2)}, u32[]{:S(2)}) collective-permute-start(bf16[256,512]{1,0:T(8,128)(2,1)S(1)} %add_convert_fusion.5.refs_8_), channel_id=1, source_target_pairs={{0,4},{2,6},{4,0},{6,2},{1,5},{3,7},{5,1},{7,3},{8,12},{10,14},{12... | collective-permute-start | bytes 786440 | tf_op jit(solution)/shard_map/ppermute | solution.py:20
  208.0 11.7 %collective-permute-start.43 = (bf16[256,512]{1,0:T(8,128)(2,1)S(1)}, bf16[256,512]{1,0:T(8,128)(2,1)S(1)}, u32[]{:S(2)}, u32[]{:S(2)}) collective-permute-start(bf16[256,512]{1,0:T(8,128)(2,1)S(1)} %add_convert_fusion.5.refs_8_), channel_id=1, source_target_pairs={{0,8},{8,0},{1,9},{9,1},{2,10},{10,2},{3,11},{11,3},{4,12},{12,4},... | collective-permute-start | bytes 786440 | tf_op jit(solution)/shard_map/ppermute | solution.py:20
  215.4 9.2 %collective-permute-start.36 = (bf16[256,512]{1,0:T(8,128)(2,1)S(1)}, bf16[256,512]{1,0:T(8,128)(2,1)S(1)}, u32[]{:S(2)}, u32[]{:S(2)}) collective-permute-start(bf16[256,512]{1,0:T(8,128)(2,1)S(1)} %add_convert_fusion.4.refs_0_), channel_id=1, source_target_pairs={{0,2},{2,4},{4,6},{6,0},{1,3},{3,5},{5,7},{7,1},{8,10},{10,12},{12... | collective-permute-start | bytes 786440 | tf_op jit(solution)/shard_map/ppermute | solution.py:20
  216.7 12.7 %collective-permute-start.37 = (bf16[256,512]{1,0:T(8,128)(2,1)S(1)}, bf16[256,512]{1,0:T(8,128)(2,1)S(1)}, u32[]{:S(2)}, u32[]{:S(2)}) collective-permute-start(bf16[256,512]{1,0:T(8,128)(2,1)S(1)} %add_convert_fusion.4.refs_0_), channel_id=1, source_target_pairs={{0,6},{2,0},{4,2},{6,4},{1,7},{3,1},{5,3},{7,5},{8,14},{10,8},{12,... | collective-permute-start | bytes 786440 | tf_op jit(solution)/shard_map/ppermute | solution.py:20
  218.6 12.0 %collective-permute-start.38 = (bf16[256,512]{1,0:T(8,128)(2,1)S(1)}, bf16[256,512]{1,0:T(8,128)(2,1)S(1)}, u32[]{:S(2)}, u32[]{:S(2)}) collective-permute-start(bf16[256,512]{1,0:T(8,128)(2,1)S(1)} %add_convert_fusion.4.refs_0_), channel_id=1, source_target_pairs={{0,4},{2,6},{4,0},{6,2},{1,5},{3,7},{5,1},{7,3},{8,12},{10,14},{12... | collective-permute-start | bytes 786440 | tf_op jit(solution)/shard_map/ppermute | solution.py:20
  219.7 10.9 %collective-permute-start.39 = (bf16[256,512]{1,0:T(8,128)(2,1)S(1)}, bf16[256,512]{1,0:T(8,128)(2,1)S(1)}, u32[]{:S(2)}, u32[]{:S(2)}) collective-permute-start(bf16[256,512]{1,0:T(8,128)(2,1)S(1)} %add_convert_fusion.4.refs_0_), channel_id=1, source_target_pairs={{0,8},{8,0},{1,9},{9,1},{2,10},{10,2},{3,11},{11,3},{4,12},{12,4},... | collective-permute-start | bytes 786440 | tf_op jit(solution)/shard_map/ppermute | solution.py:20
  219.7 11.4 %collective-permute-start.44 = (bf16[256,512]{1,0:T(8,128)(2,1)S(1)}, bf16[256,512]{1,0:T(8,128)(2,1)S(1)}, u32[]{:S(2)}, u32[]{:S(2)}) collective-permute-start(bf16[256,512]{1,0:T(8,128)(2,1)S(1)} %collective-permute-done.33.refs_9_), channel_id=1, source_target_pairs={{0,8},{8,0},{1,9},{9,1},{2,10},{10,2},{3,11},{11,3},{4,12},{12,4},... | collective-permute-start | bytes 786440 | tf_op jit(solution)/shard_map/ppermute | solution.py:20
  224.7 8.3 %collective-permute-start.45 = (bf16[256,512]{1,0:T(8,128)(2,1)S(1)}, bf16[256,512]{1,0:T(8,128)(2,1)S(1)}, u32[]{:S(2)}, u32[]{:S(2)}) collective-permute-start(bf16[256,512]{1,0:T(8,128)(2,1)S(1)} %collective-permute-done.34.refs_10_), channel_id=1, source_target_pairs={{0,8},{8,0},{1,9},{9,1},{2,10},{10,2},{3,11},{11,3},{4,12},{12,4},... | collective-permute-start | bytes 786440 | tf_op jit(solution)/shard_map/ppermute | solution.py:20
  233.0 19.8 %collective-permute-start.47 = (f32[138,512]{1,0:T(8,128)}, f32[138,512]{1,0:T(8,128)}, u32[]{:S(2)}, u32[]{:S(2)}) collective-permute-start(f32[138,512]{1,0:T(8,128)} %pad_maximum_fusion.3), channel_id=1, source_target_pairs={{1,8},{8,1},{3,10},{10,3},{5,12},{12,5},{7,14},{14,7},{17,24},{24,... | collective-permute-start | bytes 847880 | tf_op jit(solution)/shard_map/ppermute | solution.py:24
  250.6 19.5 %collective-permute-start.48 = (bf16[160,1024]{1,0:T(8,128)(2,1)}, bf16[160,1024]{1,0:T(8,128)(2,1)S(1)}, u32[]{:S(2)}, u32[]{:S(2)}) collective-permute-start(bf16[160,1024]{1,0:T(8,128)(2,1)} %get-tuple-element.109), channel_id=1, source_target_pairs={{0,1},{1,16},{16,17},{17,32},{32,33},{33,48},{48,49},{49,64},{64,6... | collective-permute-start | bytes 983048 | tf_op jit(solution)/shard_map/ppermute | solution.py:30
  288.3 9.0 %collective-permute-start.57 = (bf16[256,512]{1,0:T(8,128)(2,1)S(1)}, bf16[256,512]{1,0:T(8,128)(2,1)S(1)}, u32[]{:S(2)}, u32[]{:S(2)}) collective-permute-start(bf16[256,512]{1,0:T(8,128)(2,1)S(1)} %get-tuple-element.127), channel_id=1, source_target_pairs={{0,4},{2,6},{4,0},{6,2},{1,5},{3,7},{5,1},{7,3},{8,12},{10,14},{12... | collective-permute-start | bytes 786440 | tf_op jit(solution)/shard_map/ppermute | solution.py:20
  290.3 13.0 %collective-permute-start.56 = (bf16[256,512]{1,0:T(8,128)(2,1)S(1)}, bf16[256,512]{1,0:T(8,128)(2,1)S(1)}, u32[]{:S(2)}, u32[]{:S(2)}) collective-permute-start(bf16[256,512]{1,0:T(8,128)(2,1)S(1)} %get-tuple-element.128), channel_id=1, source_target_pairs={{0,6},{2,0},{4,2},{6,4},{1,7},{3,1},{5,3},{7,5},{8,14},{10,8},{12,... | collective-permute-start | bytes 786440 | tf_op jit(solution)/shard_map/ppermute | solution.py:20
  292.1 12.5 %collective-permute-start.55 = (bf16[256,512]{1,0:T(8,128)(2,1)S(1)}, bf16[256,512]{1,0:T(8,128)(2,1)S(1)}, u32[]{:S(2)}, u32[]{:S(2)}) collective-permute-start(bf16[256,512]{1,0:T(8,128)(2,1)S(1)} %get-tuple-element.126), channel_id=1, source_target_pairs={{0,2},{2,4},{4,6},{6,0},{1,3},{3,5},{5,7},{7,1},{8,10},{10,12},{12... | collective-permute-start | bytes 786440 | tf_op jit(solution)/shard_map/ppermute | solution.py:20
  292.5 16.1 %collective-permute-start.52 = (bf16[256,512]{1,0:T(8,128)(2,1)S(1)}, bf16[256,512]{1,0:T(8,128)(2,1)S(1)}, u32[]{:S(2)}, u32[]{:S(2)}) collective-permute-start(bf16[256,512]{1,0:T(8,128)(2,1)S(1)} %get-tuple-element.124), channel_id=1, source_target_pairs={{0,4},{2,6},{4,0},{6,2},{1,5},{3,7},{5,1},{7,3},{8,12},{10,14},{12... | collective-permute-start | bytes 786440 | tf_op jit(solution)/shard_map/ppermute | solution.py:20
  293.9 20.6 %collective-permute-start.51 = (bf16[256,512]{1,0:T(8,128)(2,1)S(1)}, bf16[256,512]{1,0:T(8,128)(2,1)S(1)}, u32[]{:S(2)}, u32[]{:S(2)}) collective-permute-start(bf16[256,512]{1,0:T(8,128)(2,1)S(1)} %get-tuple-element.125), channel_id=1, source_target_pairs={{0,6},{2,0},{4,2},{6,4},{1,7},{3,1},{5,3},{7,5},{8,14},{10,8},{12,... | collective-permute-start | bytes 786440 | tf_op jit(solution)/shard_map/ppermute | solution.py:20
  297.3 17.7 %collective-permute-start.50 = (bf16[256,512]{1,0:T(8,128)(2,1)S(1)}, bf16[256,512]{1,0:T(8,128)(2,1)S(1)}, u32[]{:S(2)}, u32[]{:S(2)}) collective-permute-start(bf16[256,512]{1,0:T(8,128)(2,1)S(1)} %get-tuple-element.123), channel_id=1, source_target_pairs={{0,2},{2,4},{4,6},{6,0},{1,3},{3,5},{5,7},{7,1},{8,10},{10,12},{12... | collective-permute-start | bytes 786440 | tf_op jit(solution)/shard_map/ppermute | solution.py:20
  304.8 12.7 %collective-permute-start.58 = (bf16[256,512]{1,0:T(8,128)(2,1)S(1)}, bf16[256,512]{1,0:T(8,128)(2,1)S(1)}, u32[]{:S(2)}, u32[]{:S(2)}) collective-permute-start(bf16[256,512]{1,0:T(8,128)(2,1)S(1)} %fusion.3), channel_id=1, source_target_pairs={{1,8},{8,1},{3,10},{10,3},{5,12},{12,5},{7,14},{14,7},{17,24},{24,... | collective-permute-start | bytes 786440 | tf_op jit(solution)/shard_map/ppermute | solution.py:24
  315.2 9.2 %collective-permute-start.53 = (bf16[256,512]{1,0:T(8,128)(2,1)S(1)}, bf16[256,512]{1,0:T(8,128)(2,1)S(1)}, u32[]{:S(2)}, u32[]{:S(2)}) collective-permute-start(bf16[256,512]{1,0:T(8,128)(2,1)S(1)} %fusion.7), channel_id=1, source_target_pairs={{1,8},{8,1},{3,10},{10,3},{5,12},{12,5},{7,14},{14,7},{17,24},{24,... | collective-permute-start | bytes 786440 | tf_op jit(solution)/shard_map/ppermute | solution.py:24
  (58 other events, 877.1 us)
Sparse Core Ops, SparseCore 0:
  9.7 87.0 all-gather.6
  108.1 98.3 all-gather.8
  208.7 58.0 all-gather.10
where the time goes:
time: 339 us; the launch traced here: 332 us
  waiting for transfers between devices  132 us (39%)
  starting transfers between devices  87.2 us (26%)
  Pallas kernels  64.3 us (19%)
  local copies, waits for them, and re-layouts  23.4 us (7%)
  between operations  14.5 us (4%)
  other arithmetic  10.6 us (3%)
    ppermute x46, waiting for transfers between devices, shift(): lax.ppermute(value, axis, [(i, (i + by) % size) for i in range(size)])  104 us
    ppermute x46, starting transfers between devices, shift(): lax.ppermute(value, axis, [(i, (i + by) % size) for i in range(size)])  42 us
    pallas_call x2, Pallas kernels, project_in(): pl.pallas_call(functools.partial(in_kernel, moves, len(pieces), halo), ou...  28.6 us
    ppermute x5, starting transfers between devices, swap(): moved = lax.ppermute(value, ('core', 'xh'), [(1, 2), (2, 1)])  17.7 us
    pallas_call x2, Pallas kernels, filtered(): pl.pallas_call(functools.partial(filter_kernel, halo, length), out_shape=...  17.5 us
    unnamed x90, local copies, waits for them, and re-layouts  13 us
    ppermute x5, waiting for transfers between devices, swap(): moved = lax.ppermute(value, ('core', 'xh'), [(1, 2), (2, 1)])  12.8 us
    pallas_call x2, Pallas kernels, mix_out(): pl.pallas_call(functools.partial(mix_kernel, moves, halo, length, len(out...  10.1 us
  transfers between devices with their start and end apart: 62, of which 29 were waited for; matrix products, arithmetic and copies ran while one was open for 6% of the time, Pallas kernels for 18%

commit v1 on v0

--- a/solution.py
+++ b/solution.py
@@ -24,6 +24,11 @@
     moved = lax.ppermute(value, ("core", "xh"), [(1, 2), (2, 1)])
     same = lax.axis_index("core") == lax.axis_index("xh")
     return jnp.where(same, value, moved)
+
+
+def shift_swapped(value, by):
+    pairs = [(a * 8 + z * 2 + b, b * 8 + (z + by) % 4 * 2 + a) for a in range(2) for z in range(4) for b in range(2)]
+    return lax.ppermute(value, ("core", "z", "xh"), pairs)
 
 
 def from_behind(value, axes):
@@ -412,25 +417,26 @@
 
     def second_z(own, theirs):
         both = (own.astype(jnp.float32) + theirs.astype(jnp.float32)).astype(jnp.bfloat16)
-        return both[0], [shift(both[at], "z", by) for by, at in ((1, 1), (-1, 3), (2, 2))]
-
-    def second_sum(own, received, rows):
-        total = rows.astype(jnp.float32) + own.astype(jnp.float32)
+        return [shift_swapped(both[at], by) for by, at in ((1, 1), (-1, 3), (2, 2))] + [swap(both[0])]
+
+    def second_sum(received, rows):
+        total = rows.astype(jnp.float32)
         for value in received:
             total = total + value.astype(jnp.float32)
-        return swap(total.astype(jnp.bfloat16))
-
+        return total.astype(jnp.bfloat16)
+
+    high, low = after((high, low), p_low)
+    high, low = swap(high), swap(low)
     inner_high = second_filter(p_low, p_high)
     inner_low = second_filter(tail, p_low)
-    inner_high, inner_low = together(inner_high, inner_low)
+    inner_high, inner_low, high, low = together(inner_high, inner_low, high, low)
     own_high, theirs_high = second_parts(inner_high)
     theirs_high = other_core(theirs_high)
-    own_high, high_z = second_z(own_high, theirs_high)
+    high_z = second_z(own_high, theirs_high)
     own_low, theirs_low = second_parts(inner_low)
-    theirs_low = other_core(theirs_low)
-    high = second_sum(own_high, high_z, high)
-    own_low, low_z = second_z(own_low, theirs_low)
-    low = second_sum(own_low, low_z, low)
+    low_z = second_z(own_low, other_core(theirs_low))
+    high = second_sum(high_z, high)
+    low = second_sum(low_z, low)
     return jnp.concatenate([low, high], axis=0)
 
 

time: 339 us -> 340 us (level)
  the two profiles are of different devices: /device:TPU:3 before, /device:TPU:1 now
where the time goes in v1:
time: 340 us; the launch traced here: 336 us
  starting transfers between devices  116 us (34%)
  waiting for transfers between devices  110 us (32%)
  Pallas kernels  61.9 us (18%)
  local copies, waits for them, and re-layouts  23.4 us (7%)
  between operations  14.3 us (4%)
  other arithmetic  9.88 us (3%)
    ppermute x40, waiting for transfers between devices, shift(): lax.ppermute(value, axis, [(i, (i + by) % size) for i in range(size)])  86.9 us
    ppermute x40, starting transfers between devices, shift(): lax.ppermute(value, axis, [(i, (i + by) % size) for i in range(size)])  41.6 us
    pallas_call x2, Pallas kernels, project_in(): pl.pallas_call(functools.partial(in_kernel, moves, len(pieces), halo), ou...  28.6 us
    ppermute x7, starting transfers between devices, swap(): moved = lax.ppermute(value, ('core', 'xh'), [(1, 2), (2, 1)])  28.4 us
    ppermute x6, starting transfers between devices, shift_swapped(): return lax.ppermute(value, ('core', 'z', 'xh'), pairs)  16.6 us
    pallas_call x2, Pallas kernels, filtered(): pl.pallas_call(functools.partial(filter_kernel, halo, length), out_shape=...  15.2 us
    unnamed x96, local copies, waits for them, and re-layouts  13.1 us
    ppermute x2, starting transfers between devices, over_z(): lax.ppermute(mine, ('core', 'xh'), [(1, 0), (2, 3)])  10.7 us
  transfers between devices with their start and end apart: 64, of which 26 were waited for; matrix products, arithmetic and copies ran while one was open for 6% of the time, Pallas kernels for 17%

profile of v1, /device:TPU:1, one launch (start us, length us, event | category | flops | bytes accessed | tf_op | source)
XLA Modules:
  0.0 335.6 jit_solution(9448978777012997943)
XLA Ops:
  10.0 2.1 collective-permute-start.1
  13.3 5.2 %collective-permute-start.2 = (bf16[256,3,512]{0,2,1:T(8,128)(2,1)}, bf16[256,3,512]{0,2,1:T(8,128)(2,1)}, u32[]{:S(2)}, u32[]{:S(2)}) collective-permute-start(bf16[256,3,512]{0,2,1:T(8,128)(2,1)} %bitcast.31), channel_id=1, source_target_pairs={{1,8},{8,1},{3,10},{10,3},{5,12},{12,5},{7,14},{14,7},{17,24},{24,... | collective-permute-start | bytes 2359304 | tf_op jit(solution)/shard_map/ppermute | solution.py:24
  23.9 16.3 %collective-permute-done.1.refs_2_.refs_1_ = bf16[256,2048]{1,0:T(8,128)(2,1)S(1)} collective-permute-done((bf16[256,2048]{1,0:T(8,128)(2,1)S(1)}, bf16[256,2048]{1,0:T(8,128)(2,1)S(1)}, u32[]{:S(2)}, u32[]{:S(2)}) %collective-permute-start.1) | collective-permute-done | bytes 1048608 | tf_op jit(solution)/shard_map/ppermute | solution.py:20
  40.2 6.4 %collective-permute-start.3 = (bf16[512,256]{1,0:T(8,128)(2,1)S(1)}, bf16[512,256]{1,0:T(8,128)(2,1)S(1)}, u32[]{:S(2)}, u32[]{:S(2)}) collective-permute-start(bf16[512,256]{1,0:T(8,128)(2,1)S(1)} %slice_bitcast_fusion.11), channel_id=1, source_target_pairs={{1,8},{8,1},{3,10},{10,3},{5,12},{12,5},{7,14},{14,7},{17,24},{24,... | collective-permute-start | bytes 786440 | tf_op jit(solution)/shard_map/ppermute | solution.py:24
  46.6 5.8 %collective-permute-done.2 = bf16[256,3,512]{0,2,1:T(8,128)(2,1)} collective-permute-done((bf16[256,3,512]{0,2,1:T(8,128)(2,1)}, bf16[256,3,512]{0,2,1:T(8,128)(2,1)}, u32[]{:S(2)}, u32[]{:S(2)}) %collective-permute-start.2) | collective-permute-done | bytes 786464 | tf_op jit(solution)/shard_map/ppermute | solution.py:24
  52.4 2.3 broadcast_select_fusion
  56.0 10.5 %collective-permute-done.6.refs_5_.refs_4_ = bf16[256,2048]{1,0:T(8,128)(2,1)} collective-permute-done((bf16[256,2048]{1,0:T(8,128)(2,1)S(1)}, bf16[256,2048]{1,0:T(8,128)(2,1)}, u32[]{:S(2)}, u32[]{:S(2)}) %collective-permute-start.6) | collective-permute-done | bytes 1048608 | tf_op jit(solution)/shard_map/ppermute | solution.py:20
  71.3 14.4 %collective-permute-done.8.refs_12_.refs_11_ = bf16[256,1280]{1,0:T(8,128)(2,1)S(1)} collective-permute-done((bf16[256,1280]{1,0:T(8,128)(2,1)S(1)}, bf16[256,1280]{1,0:T(8,128)(2,1)S(1)}, u32[]{:S(2)}, u32[]{:S(2)}) %collective-permute-start.8) | collective-permute-done | bytes 655392 | tf_op jit(solution)/shard_map/ppermute | solution.py:20
  86.3 13.2 %collective-permute-done.10.refs_14_.refs_13_ = bf16[256,1280]{1,0:T(8,128)(2,1)S(1)} collective-permute-done((bf16[256,1280]{1,0:T(8,128)(2,1)S(1)}, bf16[256,1280]{1,0:T(8,128)(2,1)S(1)}, u32[]{:S(2)}, u32[]{:S(2)}) %collective-permute-start.10) | collective-permute-done | bytes 655392 | tf_op jit(solution)/shard_map/ppermute | solution.py:20
  99.6 4.2 %collective-permute-done.7.refs_11_.refs_10_ = bf16[3,256,768]{2,1,0:T(8,128)(2,1)S(1)} collective-permute-done((bf16[3,256,768]{2,1,0:T(8,128)(2,1)S(1)}, bf16[3,256,768]{2,1,0:T(8,128)(2,1)S(1)}, u32[]{:S(2)}, u32[]{:S(2)}) %collective-permute-start.7) | collective-permute-done | bytes 1179680 | tf_op jit(solution)/shard_map/ppermute | solution.py:20
  104.0 2.6 collective-permute-done.15.refs_10_.refs_9_
  107.7 2.3 copy.14
  120.2 13.8 %shard_map.82 = (bf16[256,1536]{1,0:T(8,128)(2,1)S(1)}, bf16[256,1536]{1,0:T(8,128)(2,1)S(1)}, bf16[32,1024]{1,0:T(8,128)(2,1)S(1)}) custom-call(s32[24]{0:T(128)S(1)} %stack.128.index_ref, s32[8]{0:T(128)S(1)} %iota.3.place_ref, f32[8,512]{1,0:T(8,128)S(1)} %squeeze.43.gain_ref, bf16[8,512,512]{2,1,0:T(8,128)(2,1)} %bitcast.71, ...), custom_call_target="tpu_custom_call" | custom-call | flops 6442450944 | bytes 18874368 | tf_op jit(solution)/shard_map/pallas_call | solution.py:123
  135.3 5.5 %shard_map.84 = (bf16[256,1024]{1,0:T(8,128)(2,1)S(1)}, bf16[256,1024]{1,0:T(8,128)(2,1)}, bf16[256,1024]{1,0:T(8,128)(2,1)}, bf16[256,1024]{1,0:T(8,128)(2,1)}) custom-call(s32[24]{0:T(128)S(1)} %copy-done.24, bf16[256,1536]{1,0:T(8,128)(2,1)S(1)} %get-tuple-element.85.main_ref.before_ref, bf16[256,1536]{1,0:T(8,128)(2,1)S(1)} %get-tuple-element.90.main_ref, ...), custom_call_target="tpu_custom_call" | custom-call | flops 1073741824 | bytes 6291456 | tf_op jit(solution)/shard_map/pallas_call | solution.py:250
  140.8 3.0 collective-permute-start.26
  145.3 4.1 %collective-permute-start.20 = (bf16[32,1024]{1,0:T(8,128)(2,1)}, bf16[32,1024]{1,0:T(8,128)(2,1)S(1)}, u32[]{:S(2)}, u32[]{:S(2)}) collective-permute-start(bf16[32,1024]{1,0:T(8,128)(2,1)} %copy-done.27), channel_id=1, source_target_pairs={{0,8},{8,16},{16,24},{24,32},{32,40},{40,48},{48,56},{56,64},{64,7... | collective-permute-start | bytes 196616 | tf_op jit(solution)/shard_map/ppermute | solution.py:35
  155.6 4.4 %shard_map.83 = (bf16[256,1024]{1,0:T(8,128)(2,1)S(1)}, bf16[256,1024]{1,0:T(8,128)(2,1)S(1)}, bf16[256,1024]{1,0:T(8,128)(2,1)S(1)}, bf16[256,1024]{1,0:T(8,128)(2,1)S(1)}) custom-call(s32[24]{0:T(128)S(1)} %copy-done.25, bf16[32,1024]{1,0:T(8,128)(2,1)S(1)} %collective-permute-done.20.before_ref, bf16[256,1536]{1,0:T(8,128)(2,1)S(1)} %copy-done.5, ...), custom_call_target="tpu_custom_call" | custom-call | flops 1073741824 | bytes 6291456 | tf_op jit(solution)/shard_map/pallas_call | solution.py:250
  160.6 2.2 collective-permute-start.22
  162.8 4.8 %collective-permute-done.25 = bf16[256,1024]{1,0:T(8,128)(2,1)} collective-permute-done((bf16[256,1024]{1,0:T(8,128)(2,1)}, bf16[256,1024]{1,0:T(8,128)(2,1)}, u32[]{:S(2)}, u32[]{:S(2)}) %collective-permute-start.25) | collective-permute-done | bytes 524320 | tf_op jit(solution)/shard_map/ppermute | solution.py:20
  171.0 6.7 %collective-permute-start.28 = (bf16[256,512]{1,0:T(8,128)(2,1)S(1)}, bf16[256,512]{1,0:T(8,128)(2,1)S(1)}, u32[]{:S(2)}, u32[]{:S(2)}) collective-permute-start(bf16[256,512]{1,0:T(8,128)(2,1)S(1)} %get-tuple-element.141), channel_id=1, source_target_pairs={{1,8},{8,1},{3,10},{10,3},{5,12},{12,5},{7,14},{14,7},{17,24},{24,... | collective-permute-start | bytes 786440 | tf_op jit(solution)/shard_map/ppermute | solution.py:377
  179.7 4.7 %collective-permute-start.27 = (bf16[256,512]{1,0:T(8,128)(2,1)S(1)}, bf16[256,512]{1,0:T(8,128)(2,1)S(1)}, u32[]{:S(2)}, u32[]{:S(2)}) collective-permute-start(bf16[256,512]{1,0:T(8,128)(2,1)S(1)} %get-tuple-element.142), channel_id=1, source_target_pairs={{1,0},{8,9},{3,2},{10,11},{5,4},{12,13},{7,6},{14,15},{17,16},{24,... | collective-permute-start | bytes 786440 | tf_op jit(solution)/shard_map/ppermute | solution.py:376
  184.5 5.1 %collective-permute-done.23 = bf16[256,1024]{1,0:T(8,128)(2,1)S(1)} collective-permute-done((bf16[256,1024]{1,0:T(8,128)(2,1)S(1)}, bf16[256,1024]{1,0:T(8,128)(2,1)S(1)}, u32[]{:S(2)}, u32[]{:S(2)}) %collective-permute-start.23) | collective-permute-done | bytes 524320 | tf_op jit(solution)/shard_map/ppermute | solution.py:20
  189.6 5.4 %collective-permute-done.27 = bf16[256,512]{1,0:T(8,128)(2,1)S(1)} collective-permute-done((bf16[256,512]{1,0:T(8,128)(2,1)S(1)}, bf16[256,512]{1,0:T(8,128)(2,1)S(1)}, u32[]{:S(2)}, u32[]{:S(2)}) %collective-permute-start.27) | collective-permute-done | bytes 262176 | tf_op jit(solution)/shard_map/ppermute | solution.py:376
  195.4 2.5 collective-permute-start.31
  199.2 6.0 %collective-permute-start.30 = (bf16[256,512]{1,0:T(8,128)(2,1)S(1)}, bf16[256,512]{1,0:T(8,128)(2,1)}, u32[]{:S(2)}, u32[]{:S(2)}) collective-permute-start(bf16[256,512]{1,0:T(8,128)(2,1)S(1)} %get-tuple-element.140), channel_id=1, source_target_pairs={{1,0},{8,9},{3,2},{10,11},{5,4},{12,13},{7,6},{14,15},{17,16},{24,... | collective-permute-start | bytes 786440 | tf_op jit(solution)/shard_map/ppermute | solution.py:376
  206.2 2.0 collective-permute-start.34
  208.2 12.5 %collective-permute-start.35 = (bf16[256,512]{1,0:T(8,128)(2,1)S(1)}, bf16[256,512]{1,0:T(8,128)(2,1)S(1)}, u32[]{:S(2)}, u32[]{:S(2)}) collective-permute-start(bf16[256,512]{1,0:T(8,128)(2,1)S(1)} %add_convert_fusion.7.refs_8_), channel_id=1, source_target_pairs={{0,4},{2,6},{4,0},{6,2},{1,5},{3,7},{5,1},{7,3},{8,12},{10,14},{12... | collective-permute-start | bytes 786440 | tf_op jit(solution)/shard_map/ppermute | solution.py:20
  220.8 4.1 %collective-permute-start.47 = (f32[138,512]{1,0:T(8,128)S(1)}, f32[138,512]{1,0:T(8,128)S(1)}, u32[]{:S(2)}, u32[]{:S(2)}) collective-permute-start(f32[138,512]{1,0:T(8,128)S(1)} %pad_maximum_fusion.3), channel_id=1, source_target_pairs={{1,8},{8,1},{3,10},{10,3},{5,12},{12,5},{7,14},{14,7},{17,24},{24,... | collective-permute-start | bytes 847880 | tf_op jit(solution)/shard_map/ppermute | solution.py:24
  225.0 2.4 collective-permute-done.35.refs_11_
  228.7 2.7 collective-permute-start.37
  232.3 9.8 %collective-permute-done.36.refs_1_ = bf16[256,512]{1,0:T(8,128)(2,1)S(1)} collective-permute-done((bf16[256,512]{1,0:T(8,128)(2,1)S(1)}, bf16[256,512]{1,0:T(8,128)(2,1)S(1)}, u32[]{:S(2)}, u32[]{:S(2)}) %collective-permute-start.36) | collective-permute-done | bytes 262176 | tf_op jit(solution)/shard_map/ppermute | solution.py:20
  245.2 14.8 %shard_map.85 = (bf16[256,1536]{1,0:T(8,128)(2,1)}, bf16[256,1536]{1,0:T(8,128)(2,1)}, bf16[160,1024]{1,0:T(8,128)(2,1)}) custom-call(s32[24]{0:T(128)S(1)} %copy-done.26, s32[16]{0:T(128)S(1)} %stack.137.place_ref, f32[8,512]{1,0:T(8,128)S(1)} %squeeze.41.gain_ref, bf16[256,512]{1,0:T(8,128)(2,1)S(1)} %add_convert_fusion.6.refs_0_, ...), custom_call_target="tpu_custom_call" | custom-call | flops 6442450944 | bytes 18874368 | tf_op jit(solution)/shard_map/pallas_call | solution.py:123
  260.0 3.2 collective-permute-start.48
  263.2 4.8 %collective-permute-start.49 = (bf16[256,512]{1,0:T(8,128)(2,1)S(1)}, bf16[256,512]{1,0:T(8,128)(2,1)S(1)}, u32[]{:S(2)}, u32[]{:S(2)}) collective-permute-start(bf16[256,512]{1,0:T(8,128)(2,1)S(1)} %add_convert_fusion.7.refs_8_), channel_id=1, source_target_pairs={{1,8},{8,1},{3,10},{10,3},{5,12},{12,5},{7,14},{14,7},{17,24},{24,... | collective-permute-start | bytes 786440 | tf_op jit(solution)/shard_map/ppermute | solution.py:24
  268.1 2.3 collective-permute-start.50
  272.6 7.6 %shard_map.86.inner = bf16[256,512]{1,0:T(8,128)(2,1)S(1)} custom-call(bf16[256,1536]{1,0:T(8,128)(2,1)S(1)} %copy-done.28, bf16[256,1536]{1,0:T(8,128)(2,1)S(1)} %copy-done.29, f32[9,512]{1,0:T(8,128)S(1)} %slice.158.feat_ref, f32[128,512]{1,0:T(8,128)S(1)} %slice.159.filter_ref, f32[1,512]{1,0:T(1,128)S(1)} %slice.160.skip_ref), custom_call_target="tpu_custom_call" | custom-call | flops 3221225472 | bytes 3145728 | tf_op jit(solution)/shard_map/pallas_call | solution.py:273
  280.3 7.6 %shard_map.87.inner = bf16[256,512]{1,0:T(8,128)(2,1)S(1)} custom-call(bf16[160,1024]{1,0:T(8,128)(2,1)S(1)} %collective-permute-done.48.before_ref, bf16[256,1536]{1,0:T(8,128)(2,1)S(1)} %copy-done.28, f32[9,512]{1,0:T(8,128)S(1)} %slice.158.feat_ref, f32[128,512]{1,0:T(8,128)S(1)} %slice.159.filter_ref, f32[1,512]{1,0:T(1,128)S(1)} %slice.160.skip_ref), custom_call_target="tpu_custom_call" | custom-call | flops 3221225472 | bytes 3145728 | tf_op jit(solution)/shard_map/pallas_call | solution.py:273
  288.0 4.1 %shard_map.89 = (bf16[4,256,512]{2,1,0:T(8,128)(2,1)S(1)}, bf16[4,256,512]{2,1,0:T(8,128)(2,1)S(1)}) custom-call(s32[24]{0:T(128)S(1)} %copy-done.26, bf16[256,512]{1,0:T(8,128)(2,1)S(1)} %shard_map.86.inner, bf16[16,512,256]{2,1,0:T(8,128)(2,1)} %bitcast.67), custom_call_target="tpu_custom_call" | custom-call | flops 1073741824 | bytes 6291456 | tf_op jit(solution)/shard_map/pallas_call | solution.py:296
  292.2 4.1 %shard_map.88 = (bf16[4,256,512]{2,1,0:T(8,128)(2,1)S(1)}, bf16[4,256,512]{2,1,0:T(8,128)(2,1)S(1)}) custom-call(s32[24]{0:T(128)S(1)} %copy-done.26, bf16[256,512]{1,0:T(8,128)(2,1)S(1)} %shard_map.87.inner, bf16[16,512,256]{2,1,0:T(8,128)(2,1)} %bitcast.68), custom_call_target="tpu_custom_call" | custom-call | flops 1073741824 | bytes 6291456 | tf_op jit(solution)/shard_map/pallas_call | solution.py:296
  297.4 4.2 %collective-permute-start.59 = (bf16[256,512]{1,0:T(8,128)(2,1)S(1)}, bf16[256,512]{1,0:T(8,128)(2,1)S(1)}, u32[]{:S(2)}, u32[]{:S(2)}) collective-permute-start(bf16[256,512]{1,0:T(8,128)(2,1)S(1)} %get-tuple-element.136), channel_id=1, source_target_pairs={{0,4},{1,12},{2,6},{3,14},{4,0},{5,8},{6,2},{7,10},{8,5},{9,13},{1... | collective-permute-start | bytes 786440 | tf_op jit(solution)/shard_map/ppermute | solution.py:31
  302.9 3.0 collective-permute-start.57
  305.8 2.3 collective-permute-start.60
  308.6 4.1 %collective-permute-start.54 = (bf16[256,512]{1,0:T(8,128)(2,1)S(1)}, bf16[256,512]{1,0:T(8,128)(2,1)S(1)}, u32[]{:S(2)}, u32[]{:S(2)}) collective-permute-start(bf16[256,512]{1,0:T(8,128)(2,1)S(1)} %get-tuple-element.132), channel_id=1, source_target_pairs={{0,4},{1,12},{2,6},{3,14},{4,0},{5,8},{6,2},{7,10},{8,5},{9,13},{1... | collective-permute-start | bytes 786440 | tf_op jit(solution)/shard_map/ppermute | solution.py:31
  312.6 2.3 collective-permute-start.53
  314.9 1.9 collective-permute-start.52
  316.8 3.3 collective-permute-start.55
  322.1 3.2 collective-permute-done.52
  325.3 2.5 collective-permute-done.55
  (231 shorter events, 59.1 us)
Async XLA Ops:
  6.5 110.3 %all-gather.7.cloned.1.call-start = ((), (), s32[]{:S(2)}) async-start(), calls=%async_computation | async-start | bytes 4718592 | tf_op jit(solution)/shard_map/all_gather | solution.py:317
  7.3 238.0 %all-gather.9.cloned.1.call-start = ((), (), s32[]{:S(2)}) async-start(), calls=%async_computation.1 | async-start | bytes 13369344 | tf_op jit(solution)/shard_map/all_gather | solution.py:313
  10.0 30.2 %collective-permute-start.1 = (bf16[256,2048]{1,0:T(8,128)(2,1)S(1)}, bf16[256,2048]{1,0:T(8,128)(2,1)S(1)}, u32[]{:S(2)}, u32[]{:S(2)}) collective-permute-start(bf16[256,2048]{1,0:T(8,128)(2,1)S(1)} %pad_maximum_fusion.1.refs_1_.refs_0_), channel_id=1, source_target_pairs={{0,64},{64,0},{1,65},{65,1},{2,66},{66,2},{3,67},{67,3},{4,68},{68... | collective-permute-start | bytes 3145736 | tf_op jit(solution)/shard_map/ppermute | solution.py:20
  13.3 39.2 %collective-permute-start.2 = (bf16[256,3,512]{0,2,1:T(8,128)(2,1)}, bf16[256,3,512]{0,2,1:T(8,128)(2,1)}, u32[]{:S(2)}, u32[]{:S(2)}) collective-permute-start(bf16[256,3,512]{0,2,1:T(8,128)(2,1)} %bitcast.31), channel_id=1, source_target_pairs={{1,8},{8,1},{3,10},{10,3},{5,12},{12,5},{7,14},{14,7},{17,24},{24,... | collective-permute-start | bytes 2359304 | tf_op jit(solution)/shard_map/ppermute | solution.py:24
  18.5 37.5 %collective-permute-start.4 = (bf16[256,2048]{1,0:T(8,128)(2,1)S(1)}, bf16[256,2048]{1,0:T(8,128)(2,1)S(1)}, u32[]{:S(2)}, u32[]{:S(2)}) collective-permute-start(bf16[256,2048]{1,0:T(8,128)(2,1)S(1)} %pad_maximum_fusion.1.refs_1_.refs_0_), channel_id=1, source_target_pairs={{0,16},{16,32},{32,48},{48,0},{1,17},{17,33},{33,49},{49,1},{2,18}... | collective-permute-start | bytes 3145736 | tf_op jit(solution)/shard_map/ppermute | solution.py:20
  19.8 36.2 %collective-permute-start.5 = (bf16[256,2048]{1,0:T(8,128)(2,1)S(1)}, bf16[256,2048]{1,0:T(8,128)(2,1)}, u32[]{:S(2)}, u32[]{:S(2)}) collective-permute-start(bf16[256,2048]{1,0:T(8,128)(2,1)S(1)} %pad_maximum_fusion.1.refs_1_.refs_0_), channel_id=1, source_target_pairs={{0,48},{16,0},{32,16},{48,32},{1,49},{17,1},{33,17},{49,33},{2,50}... | collective-permute-start | bytes 3145736 | tf_op jit(solution)/shard_map/ppermute | solution.py:20
  21.3 45.1 %collective-permute-start.6 = (bf16[256,2048]{1,0:T(8,128)(2,1)S(1)}, bf16[256,2048]{1,0:T(8,128)(2,1)}, u32[]{:S(2)}, u32[]{:S(2)}) collective-permute-start(bf16[256,2048]{1,0:T(8,128)(2,1)S(1)} %pad_maximum_fusion.1.refs_1_.refs_0_), channel_id=1, source_target_pairs={{0,32},{16,48},{32,0},{48,16},{1,33},{17,49},{33,1},{49,17},{2,34}... | collective-permute-start | bytes 3145736 | tf_op jit(solution)/shard_map/ppermute | solution.py:20
  40.2 15.0 %collective-permute-start.3 = (bf16[512,256]{1,0:T(8,128)(2,1)S(1)}, bf16[512,256]{1,0:T(8,128)(2,1)S(1)}, u32[]{:S(2)}, u32[]{:S(2)}) collective-permute-start(bf16[512,256]{1,0:T(8,128)(2,1)S(1)} %slice_bitcast_fusion.11), channel_id=1, source_target_pairs={{1,8},{8,1},{3,10},{10,3},{5,12},{12,5},{7,14},{14,7},{17,24},{24,... | collective-permute-start | bytes 786440 | tf_op jit(solution)/shard_map/ppermute | solution.py:24
  67.8 35.9 %collective-permute-start.7 = (bf16[3,256,768]{2,1,0:T(8,128)(2,1)S(1)}, bf16[3,256,768]{2,1,0:T(8,128)(2,1)S(1)}, u32[]{:S(2)}, u32[]{:S(2)}) collective-permute-start(bf16[3,256,768]{2,1,0:T(8,128)(2,1)S(1)} %pad_maximum_fusion), channel_id=1, source_target_pairs={{0,64},{64,0},{1,65},{65,1},{2,66},{66,2},{3,67},{67,3},{4,68},{68... | collective-permute-start | bytes 3538952 | tf_op jit(solution)/shard_map/ppermute | solution.py:20
  68.0 17.7 %collective-permute-start.8 = (bf16[256,1280]{1,0:T(8,128)(2,1)S(1)}, bf16[256,1280]{1,0:T(8,128)(2,1)S(1)}, u32[]{:S(2)}, u32[]{:S(2)}) collective-permute-start(bf16[256,1280]{1,0:T(8,128)(2,1)S(1)} %slice.131), channel_id=1, source_target_pairs={{0,16},{16,32},{32,48},{48,0},{1,17},{17,33},{33,49},{49,1},{2,18}... | collective-permute-start | bytes 1966088 | tf_op jit(solution)/shard_map/ppermute | solution.py:20
  69.4 16.9 %collective-permute-start.9 = (bf16[256,1280]{1,0:T(8,128)(2,1)S(1)}, bf16[256,1280]{1,0:T(8,128)(2,1)S(1)}, u32[]{:S(2)}, u32[]{:S(2)}) collective-permute-start(bf16[256,1280]{1,0:T(8,128)(2,1)S(1)} %slice.131), channel_id=1, source_target_pairs={{0,48},{16,0},{32,16},{48,32},{1,49},{17,1},{33,17},{49,33},{2,50}... | collective-permute-start | bytes 1966088 | tf_op jit(solution)/shard_map/ppermute | solution.py:20
  70.7 28.8 %collective-permute-start.10 = (bf16[256,1280]{1,0:T(8,128)(2,1)S(1)}, bf16[256,1280]{1,0:T(8,128)(2,1)S(1)}, u32[]{:S(2)}, u32[]{:S(2)}) collective-permute-start(bf16[256,1280]{1,0:T(8,128)(2,1)S(1)} %slice.131), channel_id=1, source_target_pairs={{0,32},{16,48},{32,0},{48,16},{1,33},{17,49},{33,1},{49,17},{2,34}... | collective-permute-start | bytes 1966088 | tf_op jit(solution)/shard_map/ppermute | solution.py:20
  85.7 18.3 %collective-permute-start.11 = (bf16[256,2048]{1,0:T(8,128)(2,1)S(1)}, bf16[256,2048]{1,0:T(8,128)(2,1)S(1)}, u32[]{:S(2)}, u32[]{:S(2)}) collective-permute-start(bf16[256,2048]{1,0:T(8,128)(2,1)S(1)} %pad_maximum_fusion.1.refs_1_.refs_0_), channel_id=1, source_target_pairs={{0,8},{8,0},{1,9},{9,1},{2,10},{10,2},{3,11},{11,3},{4,12},{12,4},... | collective-permute-start | bytes 3145736 | tf_op jit(solution)/shard_map/ppermute | solution.py:20
  85.7 18.3 %collective-permute-start.12 = (bf16[256,2048]{1,0:T(8,128)(2,1)S(1)}, bf16[256,2048]{1,0:T(8,128)(2,1)S(1)}, u32[]{:S(2)}, u32[]{:S(2)}) collective-permute-start(bf16[256,2048]{1,0:T(8,128)(2,1)S(1)} %collective-permute-done.1.refs_2_.refs_1_), channel_id=1, source_target_pairs={{0,8},{8,0},{1,9},{9,1},{2,10},{10,2},{3,11},{11,3},{4,12},{12,4},... | collective-permute-start | bytes 3145736 | tf_op jit(solution)/shard_map/ppermute | solution.py:20
  86.3 17.7 %collective-permute-start.13 = (bf16[256,2048]{1,0:T(8,128)(2,1)S(1)}, bf16[256,2048]{1,0:T(8,128)(2,1)S(1)}, u32[]{:S(2)}, u32[]{:S(2)}) collective-permute-start(bf16[256,2048]{1,0:T(8,128)(2,1)S(1)} %collective-permute-done.4.refs_3_.refs_2_), channel_id=1, source_target_pairs={{0,8},{8,0},{1,9},{9,1},{2,10},{10,2},{3,11},{11,3},{4,12},{12,4},... | collective-permute-start | bytes 3145736 | tf_op jit(solution)/shard_map/ppermute | solution.py:20
  110.0 178.0 %all-gather.11.cloned.1.call-start = ((), (), s32[]{:S(2)}) async-start(), calls=%async_computation.2 | async-start | bytes 4456448 | tf_op jit(solution)/shard_map/all_gather | solution.py:313
  140.8 19.7 %collective-permute-start.26 = (bf16[256,1024]{1,0:T(8,128)(2,1)}, bf16[256,1024]{1,0:T(8,128)(2,1)}, u32[]{:S(2)}, u32[]{:S(2)}) collective-permute-start(bf16[256,1024]{1,0:T(8,128)(2,1)} %get-tuple-element.94), channel_id=1, source_target_pairs={{0,4},{2,6},{4,0},{6,2},{1,5},{3,7},{5,1},{7,3},{8,12},{10,14},{12... | collective-permute-start | bytes 1572872 | tf_op jit(solution)/shard_map/ppermute | solution.py:20
  143.9 23.7 %collective-permute-start.25 = (bf16[256,1024]{1,0:T(8,128)(2,1)}, bf16[256,1024]{1,0:T(8,128)(2,1)}, u32[]{:S(2)}, u32[]{:S(2)}) collective-permute-start(bf16[256,1024]{1,0:T(8,128)(2,1)} %get-tuple-element.93), channel_id=1, source_target_pairs={{0,6},{2,0},{4,2},{6,4},{1,7},{3,1},{5,3},{7,5},{8,14},{10,8},{12,... | collective-permute-start | bytes 1572872 | tf_op jit(solution)/shard_map/ppermute | solution.py:20
  144.7 24.5 %collective-permute-start.24 = (bf16[256,1024]{1,0:T(8,128)(2,1)}, bf16[256,1024]{1,0:T(8,128)(2,1)}, u32[]{:S(2)}, u32[]{:S(2)}) collective-permute-start(bf16[256,1024]{1,0:T(8,128)(2,1)} %get-tuple-element.92), channel_id=1, source_target_pairs={{0,2},{2,4},{4,6},{6,0},{1,3},{3,5},{5,7},{7,1},{8,10},{10,12},{12... | collective-permute-start | bytes 1572872 | tf_op jit(solution)/shard_map/ppermute | solution.py:20
  150.5 27.1 %collective-permute-start = (bf16[512,512]{1,0:T(8,128)(2,1)S(1)}, bf16[512,512]{1,0:T(8,128)(2,1)S(1)}, u32[]{:S(2)}, u32[]{:S(2)}) collective-permute-start(bf16[512,512]{1,0:T(8,128)(2,1)S(1)} %dynamic-slice_bitcast_fusion), channel_id=1, source_target_pairs={{0,8},{8,0},{1,9},{9,1},{2,10},{10,2},{3,11},{11,3},{4,12},{12,4},... | collective-permute-start | bytes 1572872 | tf_op jit(solution)/shard_map/ppermute | solution.py:20
  160.0 19.7 %collective-permute-start.21 = (bf16[256,1024]{1,0:T(8,128)(2,1)S(1)}, bf16[256,1024]{1,0:T(8,128)(2,1)S(1)}, u32[]{:S(2)}, u32[]{:S(2)}) collective-permute-start(bf16[256,1024]{1,0:T(8,128)(2,1)S(1)} %get-tuple-element.87), channel_id=1, source_target_pairs={{0,2},{2,4},{4,6},{6,0},{1,3},{3,5},{5,7},{7,1},{8,10},{10,12},{12... | collective-permute-start | bytes 1572872 | tf_op jit(solution)/shard_map/ppermute | solution.py:20
  160.6 23.9 %collective-permute-start.22 = (bf16[256,1024]{1,0:T(8,128)(2,1)S(1)}, bf16[256,1024]{1,0:T(8,128)(2,1)S(1)}, u32[]{:S(2)}, u32[]{:S(2)}) collective-permute-start(bf16[256,1024]{1,0:T(8,128)(2,1)S(1)} %get-tuple-element.88), channel_id=1, source_target_pairs={{0,6},{2,0},{4,2},{6,4},{1,7},{3,1},{5,3},{7,5},{8,14},{10,8},{12,... | collective-permute-start | bytes 1572872 | tf_op jit(solution)/shard_map/ppermute | solution.py:20
  167.6 22.0 %collective-permute-start.23 = (bf16[256,1024]{1,0:T(8,128)(2,1)S(1)}, bf16[256,1024]{1,0:T(8,128)(2,1)S(1)}, u32[]{:S(2)}, u32[]{:S(2)}) collective-permute-start(bf16[256,1024]{1,0:T(8,128)(2,1)S(1)} %get-tuple-element.89), channel_id=1, source_target_pairs={{0,4},{2,6},{4,0},{6,2},{1,5},{3,7},{5,1},{7,3},{8,12},{10,14},{12... | collective-permute-start | bytes 1572872 | tf_op jit(solution)/shard_map/ppermute | solution.py:20
  171.0 24.0 %collective-permute-start.28 = (bf16[256,512]{1,0:T(8,128)(2,1)S(1)}, bf16[256,512]{1,0:T(8,128)(2,1)S(1)}, u32[]{:S(2)}, u32[]{:S(2)}) collective-permute-start(bf16[256,512]{1,0:T(8,128)(2,1)S(1)} %get-tuple-element.141), channel_id=1, source_target_pairs={{1,8},{8,1},{3,10},{10,3},{5,12},{12,5},{7,14},{14,7},{17,24},{24,... | collective-permute-start | bytes 786440 | tf_op jit(solution)/shard_map/ppermute | solution.py:377
  177.7 17.3 %collective-permute-start.29 = (bf16[256,512]{1,0:T(8,128)(2,1)S(1)}, bf16[256,512]{1,0:T(8,128)(2,1)S(1)}, u32[]{:S(2)}, u32[]{:S(2)}) collective-permute-start(bf16[256,512]{1,0:T(8,128)(2,1)S(1)} %get-tuple-element.141), channel_id=1, source_target_pairs={{0,8},{9,1},{2,10},{11,3},{4,12},{13,5},{6,14},{15,7},{16,24},{25,... | collective-permute-start | bytes 786440 | tf_op jit(solution)/shard_map/ppermute | solution.py:378
  179.7 15.3 %collective-permute-start.27 = (bf16[256,512]{1,0:T(8,128)(2,1)S(1)}, bf16[256,512]{1,0:T(8,128)(2,1)S(1)}, u32[]{:S(2)}, u32[]{:S(2)}) collective-permute-start(bf16[256,512]{1,0:T(8,128)(2,1)S(1)} %get-tuple-element.142), channel_id=1, source_target_pairs={{1,0},{8,9},{3,2},{10,11},{5,4},{12,13},{7,6},{14,15},{17,16},{24,... | collective-permute-start | bytes 786440 | tf_op jit(solution)/shard_map/ppermute | solution.py:376
  195.4 29.5 %collective-permute-start.31 = (bf16[256,512]{1,0:T(8,128)(2,1)S(1)}, bf16[256,512]{1,0:T(8,128)(2,1)S(1)}, u32[]{:S(2)}, u32[]{:S(2)}) collective-permute-start(bf16[256,512]{1,0:T(8,128)(2,1)S(1)} %get-tuple-element.139), channel_id=1, source_target_pairs={{1,8},{8,1},{3,10},{10,3},{5,12},{12,5},{7,14},{14,7},{17,24},{24,... | collective-permute-start | bytes 786440 | tf_op jit(solution)/shard_map/ppermute | solution.py:377
  199.2 21.5 %collective-permute-start.30 = (bf16[256,512]{1,0:T(8,128)(2,1)S(1)}, bf16[256,512]{1,0:T(8,128)(2,1)}, u32[]{:S(2)}, u32[]{:S(2)}) collective-permute-start(bf16[256,512]{1,0:T(8,128)(2,1)S(1)} %get-tuple-element.140), channel_id=1, source_target_pairs={{1,0},{8,9},{3,2},{10,11},{5,4},{12,13},{7,6},{14,15},{17,16},{24,... | collective-permute-start | bytes 786440 | tf_op jit(solution)/shard_map/ppermute | solution.py:376
  205.4 19.6 %collective-permute-start.33 = (bf16[256,512]{1,0:T(8,128)(2,1)S(1)}, bf16[256,512]{1,0:T(8,128)(2,1)S(1)}, u32[]{:S(2)}, u32[]{:S(2)}) collective-permute-start(bf16[256,512]{1,0:T(8,128)(2,1)S(1)} %add_convert_fusion.7.refs_8_), channel_id=1, source_target_pairs={{0,2},{2,4},{4,6},{6,0},{1,3},{3,5},{5,7},{7,1},{8,10},{10,12},{12... | collective-permute-start | bytes 786440 | tf_op jit(solution)/shard_map/ppermute | solution.py:20
  206.2 18.8 %collective-permute-start.34 = (bf16[256,512]{1,0:T(8,128)(2,1)S(1)}, bf16[256,512]{1,0:T(8,128)(2,1)S(1)}, u32[]{:S(2)}, u32[]{:S(2)}) collective-permute-start(bf16[256,512]{1,0:T(8,128)(2,1)S(1)} %add_convert_fusion.7.refs_8_), channel_id=1, source_target_pairs={{0,6},{2,0},{4,2},{6,4},{1,7},{3,1},{5,3},{7,5},{8,14},{10,8},{12,... | collective-permute-start | bytes 786440 | tf_op jit(solution)/shard_map/ppermute | solution.py:20
  208.2 19.3 %collective-permute-start.35 = (bf16[256,512]{1,0:T(8,128)(2,1)S(1)}, bf16[256,512]{1,0:T(8,128)(2,1)S(1)}, u32[]{:S(2)}, u32[]{:S(2)}) collective-permute-start(bf16[256,512]{1,0:T(8,128)(2,1)S(1)} %add_convert_fusion.7.refs_8_), channel_id=1, source_target_pairs={{0,4},{2,6},{4,0},{6,2},{1,5},{3,7},{5,1},{7,3},{8,12},{10,14},{12... | collective-permute-start | bytes 786440 | tf_op jit(solution)/shard_map/ppermute | solution.py:20
  220.8 11.0 %collective-permute-start.47 = (f32[138,512]{1,0:T(8,128)S(1)}, f32[138,512]{1,0:T(8,128)S(1)}, u32[]{:S(2)}, u32[]{:S(2)}) collective-permute-start(f32[138,512]{1,0:T(8,128)S(1)} %pad_maximum_fusion.3), channel_id=1, source_target_pairs={{1,8},{8,1},{3,10},{10,3},{5,12},{12,5},{7,14},{14,7},{17,24},{24,... | collective-permute-start | bytes 847880 | tf_op jit(solution)/shard_map/ppermute | solution.py:24
  228.6 13.4 %collective-permute-start.36 = (bf16[256,512]{1,0:T(8,128)(2,1)S(1)}, bf16[256,512]{1,0:T(8,128)(2,1)S(1)}, u32[]{:S(2)}, u32[]{:S(2)}) collective-permute-start(bf16[256,512]{1,0:T(8,128)(2,1)S(1)} %add_convert_fusion.6.refs_0_), channel_id=1, source_target_pairs={{0,2},{2,4},{4,6},{6,0},{1,3},{3,5},{5,7},{7,1},{8,10},{10,12},{12... | collective-permute-start | bytes 786440 | tf_op jit(solution)/shard_map/ppermute | solution.py:20
  228.7 13.4 %collective-permute-start.37 = (bf16[256,512]{1,0:T(8,128)(2,1)S(1)}, bf16[256,512]{1,0:T(8,128)(2,1)S(1)}, u32[]{:S(2)}, u32[]{:S(2)}) collective-permute-start(bf16[256,512]{1,0:T(8,128)(2,1)S(1)} %add_convert_fusion.6.refs_0_), channel_id=1, source_target_pairs={{0,6},{2,0},{4,2},{6,4},{1,7},{3,1},{5,3},{7,5},{8,14},{10,8},{12,... | collective-permute-start | bytes 786440 | tf_op jit(solution)/shard_map/ppermute | solution.py:20
  231.4 11.2 %collective-permute-start.38 = (bf16[256,512]{1,0:T(8,128)(2,1)S(1)}, bf16[256,512]{1,0:T(8,128)(2,1)S(1)}, u32[]{:S(2)}, u32[]{:S(2)}) collective-permute-start(bf16[256,512]{1,0:T(8,128)(2,1)S(1)} %add_convert_fusion.6.refs_0_), channel_id=1, source_target_pairs={{0,4},{2,6},{4,0},{6,2},{1,5},{3,7},{5,1},{7,3},{8,12},{10,14},{12... | collective-permute-start | bytes 786440 | tf_op jit(solution)/shard_map/ppermute | solution.py:20
  231.8 10.9 %collective-permute-start.39 = (bf16[256,512]{1,0:T(8,128)(2,1)S(1)}, bf16[256,512]{1,0:T(8,128)(2,1)S(1)}, u32[]{:S(2)}, u32[]{:S(2)}) collective-permute-start(bf16[256,512]{1,0:T(8,128)(2,1)S(1)} %add_convert_fusion.6.refs_0_), channel_id=1, source_target_pairs={{0,8},{8,0},{1,9},{9,1},{2,10},{10,2},{3,11},{11,3},{4,12},{12,4},... | collective-permute-start | bytes 786440 | tf_op jit(solution)/shard_map/ppermute | solution.py:20
  231.8 11.3 %collective-permute-start.44 = (bf16[256,512]{1,0:T(8,128)(2,1)S(1)}, bf16[256,512]{1,0:T(8,128)(2,1)S(1)}, u32[]{:S(2)}, u32[]{:S(2)}) collective-permute-start(bf16[256,512]{1,0:T(8,128)(2,1)S(1)} %collective-permute-done.33.refs_9_), channel_id=1, source_target_pairs={{0,8},{8,0},{1,9},{9,1},{2,10},{10,2},{3,11},{11,3},{4,12},{12,4},... | collective-permute-start | bytes 786440 | tf_op jit(solution)/shard_map/ppermute | solution.py:20
  260.0 20.3 %collective-permute-start.48 = (bf16[160,1024]{1,0:T(8,128)(2,1)}, bf16[160,1024]{1,0:T(8,128)(2,1)S(1)}, u32[]{:S(2)}, u32[]{:S(2)}) collective-permute-start(bf16[160,1024]{1,0:T(8,128)(2,1)} %get-tuple-element.113), channel_id=1, source_target_pairs={{0,1},{1,16},{16,17},{17,32},{32,33},{33,48},{48,49},{49,64},{64,6... | collective-permute-start | bytes 983048 | tf_op jit(solution)/shard_map/ppermute | solution.py:35
  263.2 17.0 %collective-permute-start.49 = (bf16[256,512]{1,0:T(8,128)(2,1)S(1)}, bf16[256,512]{1,0:T(8,128)(2,1)S(1)}, u32[]{:S(2)}, u32[]{:S(2)}) collective-permute-start(bf16[256,512]{1,0:T(8,128)(2,1)S(1)} %add_convert_fusion.7.refs_8_), channel_id=1, source_target_pairs={{1,8},{8,1},{3,10},{10,3},{5,12},{12,5},{7,14},{14,7},{17,24},{24,... | collective-permute-start | bytes 786440 | tf_op jit(solution)/shard_map/ppermute | solution.py:24
  268.1 12.2 %collective-permute-start.50 = (bf16[256,512]{1,0:T(8,128)(2,1)S(1)}, bf16[256,512]{1,0:T(8,128)(2,1)S(1)}, u32[]{:S(2)}, u32[]{:S(2)}) collective-permute-start(bf16[256,512]{1,0:T(8,128)(2,1)S(1)} %add_convert_fusion.6.refs_0_), channel_id=1, source_target_pairs={{1,8},{8,1},{3,10},{10,3},{5,12},{12,5},{7,14},{14,7},{17,24},{24,... | collective-permute-start | bytes 786440 | tf_op jit(solution)/shard_map/ppermute | solution.py:24
  296.2 11.9 %collective-permute-start.51 = (bf16[4,256,512]{2,1,0:T(8,128)(2,1)S(1)}, bf16[4,256,512]{2,1,0:T(8,128)(2,1)S(1)}, u32[]{:S(2)}, u32[]{:S(2)}) collective-permute-start(bf16[4,256,512]{2,1,0:T(8,128)(2,1)S(1)} %get-tuple-element.120), channel_id=1, source_target_pairs={{0,8},{8,0},{1,9},{9,1},{2,10},{10,2},{3,11},{11,3},{4,12},{12,4},... | collective-permute-start | bytes 3145736 | tf_op jit(solution)/shard_map/ppermute | solution.py:20
  297.4 15.2 %collective-permute-start.59 = (bf16[256,512]{1,0:T(8,128)(2,1)S(1)}, bf16[256,512]{1,0:T(8,128)(2,1)S(1)}, u32[]{:S(2)}, u32[]{:S(2)}) collective-permute-start(bf16[256,512]{1,0:T(8,128)(2,1)S(1)} %get-tuple-element.136), channel_id=1, source_target_pairs={{0,4},{1,12},{2,6},{3,14},{4,0},{5,8},{6,2},{7,10},{8,5},{9,13},{1... | collective-permute-start | bytes 786440 | tf_op jit(solution)/shard_map/ppermute | solution.py:31
  301.7 13.2 %collective-permute-start.58 = (bf16[256,512]{1,0:T(8,128)(2,1)S(1)}, bf16[256,512]{1,0:T(8,128)(2,1)S(1)}, u32[]{:S(2)}, u32[]{:S(2)}) collective-permute-start(bf16[256,512]{1,0:T(8,128)(2,1)S(1)} %get-tuple-element.137), channel_id=1, source_target_pairs={{0,6},{1,14},{2,0},{3,8},{4,2},{5,10},{6,4},{7,12},{8,7},{9,15},{1... | collective-permute-start | bytes 786440 | tf_op jit(solution)/shard_map/ppermute | solution.py:31
  302.9 13.9 %collective-permute-start.57 = (bf16[256,512]{1,0:T(8,128)(2,1)S(1)}, bf16[256,512]{1,0:T(8,128)(2,1)S(1)}, u32[]{:S(2)}, u32[]{:S(2)}) collective-permute-start(bf16[256,512]{1,0:T(8,128)(2,1)S(1)} %get-tuple-element.138), channel_id=1, source_target_pairs={{0,2},{1,10},{2,4},{3,12},{4,6},{5,14},{6,0},{7,8},{8,3},{9,11},{1... | collective-permute-start | bytes 786440 | tf_op jit(solution)/shard_map/ppermute | solution.py:31
  305.8 14.3 %collective-permute-start.60 = (bf16[256,512]{1,0:T(8,128)(2,1)S(1)}, bf16[256,512]{1,0:T(8,128)(2,1)S(1)}, u32[]{:S(2)}, u32[]{:S(2)}) collective-permute-start(bf16[256,512]{1,0:T(8,128)(2,1)S(1)} %get-tuple-element.135), channel_id=1, source_target_pairs={{1,8},{8,1},{3,10},{10,3},{5,12},{12,5},{7,14},{14,7},{17,24},{24,... | collective-permute-start | bytes 786440 | tf_op jit(solution)/shard_map/ppermute | solution.py:24
  308.6 11.9 %collective-permute-start.54 = (bf16[256,512]{1,0:T(8,128)(2,1)S(1)}, bf16[256,512]{1,0:T(8,128)(2,1)S(1)}, u32[]{:S(2)}, u32[]{:S(2)}) collective-permute-start(bf16[256,512]{1,0:T(8,128)(2,1)S(1)} %get-tuple-element.132), channel_id=1, source_target_pairs={{0,4},{1,12},{2,6},{3,14},{4,0},{5,8},{6,2},{7,10},{8,5},{9,13},{1... | collective-permute-start | bytes 786440 | tf_op jit(solution)/shard_map/ppermute | solution.py:31
  314.9 10.4 %collective-permute-start.52 = (bf16[256,512]{1,0:T(8,128)(2,1)S(1)}, bf16[256,512]{1,0:T(8,128)(2,1)S(1)}, u32[]{:S(2)}, u32[]{:S(2)}) collective-permute-start(bf16[256,512]{1,0:T(8,128)(2,1)S(1)} %get-tuple-element.134), channel_id=1, source_target_pairs={{0,2},{1,10},{2,4},{3,12},{4,6},{5,14},{6,0},{7,8},{8,3},{9,11},{1... | collective-permute-start | bytes 786440 | tf_op jit(solution)/shard_map/ppermute | solution.py:31
  316.8 11.0 %collective-permute-start.55 = (bf16[256,512]{1,0:T(8,128)(2,1)S(1)}, bf16[256,512]{1,0:T(8,128)(2,1)S(1)}, u32[]{:S(2)}, u32[]{:S(2)}) collective-permute-start(bf16[256,512]{1,0:T(8,128)(2,1)S(1)} %get-tuple-element.131), channel_id=1, source_target_pairs={{1,8},{8,1},{3,10},{10,3},{5,12},{12,5},{7,14},{14,7},{17,24},{24,... | collective-permute-start | bytes 786440 | tf_op jit(solution)/shard_map/ppermute | solution.py:24
  (63 other events, 927.2 us)
Sparse Core Ops, SparseCore 0:
  9.7 88.9 all-gather.6
  110.1 98.4 all-gather.8
  210.8 53.6 all-gather.10

commit v2 on v1

--- a/solution.py
+++ b/solution.py
@@ -425,7 +425,7 @@
             total = total + value.astype(jnp.float32)
         return total.astype(jnp.bfloat16)
 
-    high, low = after((high, low), p_low)
+    high, low = after((high, low), *low_far)
     high, low = swap(high), swap(low)
     inner_high = second_filter(p_low, p_high)
     inner_low = second_filter(tail, p_low)

time: 340 us -> 353 us (1.038)
  waiting for transfers between devices: 110 us -> 122 us
  starting transfers between devices: 116 us -> 111 us
  local copies, waits for them, and re-layouts: 23.4 us -> 28.3 us
    ppermute x7, waiting for transfers between devices: 9.21 us -> 17.8 us  [swap(): moved = lax.ppermute(value, ('core', 'xh'), [(1, 2), (2, 1)])]
    ppermute x40, waiting for transfers between devices: 86.9 us -> 92.5 us  [shift(): lax.ppermute(value, axis, [(i, (i + by) % size) for i in range(size)])]
    unnamed x96 -> x106, local copies, waits for them, and re-layouts: 13.1 us -> 18 us
  transfers between devices with their start and end apart: 64 -> 64, of which waited for: 26 -> 26; matrix products, arithmetic and copies ran while one was open for 6% -> 6% of each run, Pallas kernels for 17% -> 16%
where the time goes in v2:
time: 353 us; the launch traced here: 349 us
  waiting for transfers between devices  122 us (35%)
  starting transfers between devices  111 us (31%)
  Pallas kernels  61.6 us (17%)
  local copies, waits for them, and re-layouts  28.3 us (8%)
  between operations  14.4 us (4%)
  other arithmetic  11.6 us (3%)
    ppermute x40, waiting for transfers between devices, shift(): lax.ppermute(value, axis, [(i, (i + by) % size) for i in range(size)])  92.5 us
    ppermute x40, starting transfers between devices, shift(): lax.ppermute(value, axis, [(i, (i + by) % size) for i in range(size)])  43.5 us
    pallas_call x2, Pallas kernels, project_in(): pl.pallas_call(functools.partial(in_kernel, moves, len(pieces), halo), ou...  28.3 us
    ppermute x7, starting transfers between devices, swap(): moved = lax.ppermute(value, ('core', 'xh'), [(1, 2), (2, 1)])  26.3 us
    unnamed x106, local copies, waits for them, and re-layouts  18 us
    ppermute x7, waiting for transfers between devices, swap(): moved = lax.ppermute(value, ('core', 'xh'), [(1, 2), (2, 1)])  17.8 us
    ppermute x6, starting transfers between devices, shift_swapped(): return lax.ppermute(value, ('core', 'z', 'xh'), pairs)  15.8 us
    pallas_call x2, Pallas kernels, filtered(): pl.pallas_call(functools.partial(filter_kernel, halo, length), out_shape=...  15.2 us
  transfers between devices with their start and end apart: 64, of which 26 were waited for; matrix products, arithmetic and copies ran while one was open for 6% of the time, Pallas kernels for 16%

profile of v2, /device:TPU:1, one launch (start us, length us, event | category | flops | bytes accessed | tf_op | source)
XLA Modules:
  0.0 349.4 jit_solution(3140022424541406578)
XLA Ops:
  10.0 2.1 collective-permute-start.1
  13.3 5.2 %collective-permute-start.2 = (bf16[256,3,512]{0,2,1:T(8,128)(2,1)}, bf16[256,3,512]{0,2,1:T(8,128)(2,1)}, u32[]{:S(2)}, u32[]{:S(2)}) collective-permute-start(bf16[256,3,512]{0,2,1:T(8,128)(2,1)} %bitcast.31), channel_id=1, source_target_pairs={{1,8},{8,1},{3,10},{10,3},{5,12},{12,5},{7,14},{14,7},{17,24},{24,... | collective-permute-start | bytes 2359304 | tf_op jit(solution)/shard_map/ppermute | solution.py:24
  23.9 16.3 %collective-permute-done.1.refs_2_.refs_1_ = bf16[256,2048]{1,0:T(8,128)(2,1)S(1)} collective-permute-done((bf16[256,2048]{1,0:T(8,128)(2,1)S(1)}, bf16[256,2048]{1,0:T(8,128)(2,1)S(1)}, u32[]{:S(2)}, u32[]{:S(2)}) %collective-permute-start.1) | collective-permute-done | bytes 1048608 | tf_op jit(solution)/shard_map/ppermute | solution.py:20
  40.2 6.4 %collective-permute-start.3 = (bf16[512,256]{1,0:T(8,128)(2,1)S(1)}, bf16[512,256]{1,0:T(8,128)(2,1)S(1)}, u32[]{:S(2)}, u32[]{:S(2)}) collective-permute-start(bf16[512,256]{1,0:T(8,128)(2,1)S(1)} %slice_bitcast_fusion.11), channel_id=1, source_target_pairs={{1,8},{8,1},{3,10},{10,3},{5,12},{12,5},{7,14},{14,7},{17,24},{24,... | collective-permute-start | bytes 786440 | tf_op jit(solution)/shard_map/ppermute | solution.py:24
  46.6 5.8 %collective-permute-done.2 = bf16[256,3,512]{0,2,1:T(8,128)(2,1)} collective-permute-done((bf16[256,3,512]{0,2,1:T(8,128)(2,1)}, bf16[256,3,512]{0,2,1:T(8,128)(2,1)}, u32[]{:S(2)}, u32[]{:S(2)}) %collective-permute-start.2) | collective-permute-done | bytes 786464 | tf_op jit(solution)/shard_map/ppermute | solution.py:24
  52.4 2.3 broadcast_select_fusion
  56.0 10.4 %collective-permute-done.6.refs_5_.refs_4_ = bf16[256,2048]{1,0:T(8,128)(2,1)} collective-permute-done((bf16[256,2048]{1,0:T(8,128)(2,1)S(1)}, bf16[256,2048]{1,0:T(8,128)(2,1)}, u32[]{:S(2)}, u32[]{:S(2)}) %collective-permute-start.6) | collective-permute-done | bytes 1048608 | tf_op jit(solution)/shard_map/ppermute | solution.py:20
  71.9 13.7 %collective-permute-done.8.refs_12_.refs_11_ = bf16[256,1280]{1,0:T(8,128)(2,1)S(1)} collective-permute-done((bf16[256,1280]{1,0:T(8,128)(2,1)S(1)}, bf16[256,1280]{1,0:T(8,128)(2,1)S(1)}, u32[]{:S(2)}, u32[]{:S(2)}) %collective-permute-start.8) | collective-permute-done | bytes 655392 | tf_op jit(solution)/shard_map/ppermute | solution.py:20
  86.2 13.3 %collective-permute-done.10.refs_14_.refs_13_ = bf16[256,1280]{1,0:T(8,128)(2,1)S(1)} collective-permute-done((bf16[256,1280]{1,0:T(8,128)(2,1)S(1)}, bf16[256,1280]{1,0:T(8,128)(2,1)S(1)}, u32[]{:S(2)}, u32[]{:S(2)}) %collective-permute-start.10) | collective-permute-done | bytes 655392 | tf_op jit(solution)/shard_map/ppermute | solution.py:20
  100.3 3.4 collective-permute-done.7.refs_11_.refs_10_
  104.0 2.4 collective-permute-done.11.refs_6_.refs_5_
  107.5 2.3 copy.14
  119.9 13.8 %shard_map.82 = (bf16[256,1536]{1,0:T(8,128)(2,1)S(1)}, bf16[256,1536]{1,0:T(8,128)(2,1)S(1)}, bf16[32,1024]{1,0:T(8,128)(2,1)S(1)}) custom-call(s32[24]{0:T(128)S(1)} %stack.128.index_ref, s32[8]{0:T(128)S(1)} %iota.3.place_ref, f32[8,512]{1,0:T(8,128)S(1)} %squeeze.43.gain_ref, bf16[8,512,512]{2,1,0:T(8,128)(2,1)} %bitcast.71, ...), custom_call_target="tpu_custom_call" | custom-call | flops 6442450944 | bytes 18874368 | tf_op jit(solution)/shard_map/pallas_call | solution.py:123
  135.1 5.5 %shard_map.84 = (bf16[256,1024]{1,0:T(8,128)(2,1)S(1)}, bf16[256,1024]{1,0:T(8,128)(2,1)}, bf16[256,1024]{1,0:T(8,128)(2,1)}, bf16[256,1024]{1,0:T(8,128)(2,1)}) custom-call(s32[24]{0:T(128)S(1)} %copy-done.24, bf16[256,1536]{1,0:T(8,128)(2,1)S(1)} %get-tuple-element.85.main_ref.before_ref, bf16[256,1536]{1,0:T(8,128)(2,1)S(1)} %get-tuple-element.90.main_ref, ...), custom_call_target="tpu_custom_call" | custom-call | flops 1073741824 | bytes 6291456 | tf_op jit(solution)/shard_map/pallas_call | solution.py:250
  145.1 4.1 %collective-permute-start.20 = (bf16[32,1024]{1,0:T(8,128)(2,1)}, bf16[32,1024]{1,0:T(8,128)(2,1)S(1)}, u32[]{:S(2)}, u32[]{:S(2)}) collective-permute-start(bf16[32,1024]{1,0:T(8,128)(2,1)} %copy-done.33), channel_id=1, source_target_pairs={{0,8},{8,16},{16,24},{24,32},{32,40},{40,48},{48,56},{56,64},{64,7... | collective-permute-start | bytes 196616 | tf_op jit(solution)/shard_map/ppermute | solution.py:35
  155.3 4.4 %shard_map.83 = (bf16[256,1024]{1,0:T(8,128)(2,1)S(1)}, bf16[256,1024]{1,0:T(8,128)(2,1)S(1)}, bf16[256,1024]{1,0:T(8,128)(2,1)S(1)}, bf16[256,1024]{1,0:T(8,128)(2,1)S(1)}) custom-call(s32[24]{0:T(128)S(1)} %copy-done.25, bf16[32,1024]{1,0:T(8,128)(2,1)S(1)} %collective-permute-done.20.before_ref, bf16[256,1536]{1,0:T(8,128)(2,1)S(1)} %copy-done.5, ...), custom_call_target="tpu_custom_call" | custom-call | flops 1073741824 | bytes 6291456 | tf_op jit(solution)/shard_map/pallas_call | solution.py:250
  160.3 2.2 collective-permute-start.22
  162.5 5.4 %collective-permute-done.26 = bf16[256,1024]{1,0:T(8,128)(2,1)} collective-permute-done((bf16[256,1024]{1,0:T(8,128)(2,1)}, bf16[256,1024]{1,0:T(8,128)(2,1)}, u32[]{:S(2)}, u32[]{:S(2)}) %collective-permute-start.26) | collective-permute-done | bytes 524320 | tf_op jit(solution)/shard_map/ppermute | solution.py:20
  167.9 1.8 add_convert_fusion.3
  169.8 6.4 %collective-permute-start.28 = (bf16[256,512]{1,0:T(8,128)(2,1)S(1)}, bf16[256,512]{1,0:T(8,128)(2,1)S(1)}, u32[]{:S(2)}, u32[]{:S(2)}) collective-permute-start(bf16[256,512]{1,0:T(8,128)(2,1)S(1)} %get-tuple-element.141), channel_id=1, source_target_pairs={{1,8},{8,1},{3,10},{10,3},{5,12},{12,5},{7,14},{14,7},{17,24},{24,... | collective-permute-start | bytes 786440 | tf_op jit(solution)/shard_map/ppermute | solution.py:377
  177.5 3.0 collective-permute-done.21
  180.5 4.7 %collective-permute-start.27 = (bf16[256,512]{1,0:T(8,128)(2,1)S(1)}, bf16[256,512]{1,0:T(8,128)(2,1)S(1)}, u32[]{:S(2)}, u32[]{:S(2)}) collective-permute-start(bf16[256,512]{1,0:T(8,128)(2,1)S(1)} %get-tuple-element.142), channel_id=1, source_target_pairs={{1,0},{8,9},{3,2},{10,11},{5,4},{12,13},{7,6},{14,15},{17,16},{24,... | collective-permute-start | bytes 786440 | tf_op jit(solution)/shard_map/ppermute | solution.py:376
  185.3 4.9 %collective-permute-done.23 = bf16[256,1024]{1,0:T(8,128)(2,1)S(1)} collective-permute-done((bf16[256,1024]{1,0:T(8,128)(2,1)S(1)}, bf16[256,1024]{1,0:T(8,128)(2,1)S(1)}, u32[]{:S(2)}, u32[]{:S(2)}) %collective-permute-start.23) | collective-permute-done | bytes 524320 | tf_op jit(solution)/shard_map/ppermute | solution.py:20
  190.3 3.8 %collective-permute-done.27 = bf16[256,512]{1,0:T(8,128)(2,1)S(1)} collective-permute-done((bf16[256,512]{1,0:T(8,128)(2,1)S(1)}, bf16[256,512]{1,0:T(8,128)(2,1)S(1)}, u32[]{:S(2)}, u32[]{:S(2)}) %collective-permute-start.27) | collective-permute-done | bytes 262176 | tf_op jit(solution)/shard_map/ppermute | solution.py:376
  196.0 2.9 collective-permute-start.31
  199.0 3.5 collective-permute-start.30
  203.3 2.1 collective-permute-start.34
  205.4 12.3 %collective-permute-start.35 = (bf16[256,512]{1,0:T(8,128)(2,1)S(1)}, bf16[256,512]{1,0:T(8,128)(2,1)S(1)}, u32[]{:S(2)}, u32[]{:S(2)}) collective-permute-start(bf16[256,512]{1,0:T(8,128)(2,1)S(1)} %add_convert_fusion.7.refs_8_), channel_id=1, source_target_pairs={{0,4},{2,6},{4,0},{6,2},{1,5},{3,7},{5,1},{7,3},{8,12},{10,14},{12... | collective-permute-start | bytes 786440 | tf_op jit(solution)/shard_map/ppermute | solution.py:20
  217.7 8.0 %collective-permute-done.35.refs_11_ = bf16[256,512]{1,0:T(8,128)(2,1)S(1)} collective-permute-done((bf16[256,512]{1,0:T(8,128)(2,1)S(1)}, bf16[256,512]{1,0:T(8,128)(2,1)S(1)}, u32[]{:S(2)}, u32[]{:S(2)}) %collective-permute-start.35) | collective-permute-done | bytes 262176 | tf_op jit(solution)/shard_map/ppermute | solution.py:20
  226.0 2.7 collective-permute-start.37
  228.7 4.3 %collective-permute-start.47 = (f32[138,512]{1,0:T(8,128)S(1)}, f32[138,512]{1,0:T(8,128)}, u32[]{:S(2)}, u32[]{:S(2)}) collective-permute-start(f32[138,512]{1,0:T(8,128)S(1)} %pad_maximum_fusion.3), channel_id=1, source_target_pairs={{1,8},{8,1},{3,10},{10,3},{5,12},{12,5},{7,14},{14,7},{17,24},{24,... | collective-permute-start | bytes 847880 | tf_op jit(solution)/shard_map/ppermute | solution.py:24
  233.1 7.3 %collective-permute-done.36.refs_1_ = bf16[256,512]{1,0:T(8,128)(2,1)S(1)} collective-permute-done((bf16[256,512]{1,0:T(8,128)(2,1)S(1)}, bf16[256,512]{1,0:T(8,128)(2,1)S(1)}, u32[]{:S(2)}, u32[]{:S(2)}) %collective-permute-start.36) | collective-permute-done | bytes 262176 | tf_op jit(solution)/shard_map/ppermute | solution.py:20
  242.7 1.9 collective-permute-start.50
  246.9 10.4 %collective-permute-done.50 = bf16[256,512]{1,0:T(8,128)(2,1)} collective-permute-done((bf16[256,512]{1,0:T(8,128)(2,1)S(1)}, bf16[256,512]{1,0:T(8,128)(2,1)}, u32[]{:S(2)}, u32[]{:S(2)}) %collective-permute-start.50) | collective-permute-done | bytes 262176 | tf_op jit(solution)/shard_map/ppermute | solution.py:24
  257.3 1.9 collective-permute-start.49
  265.9 14.5 %shard_map.85 = (bf16[256,1536]{1,0:T(8,128)(2,1)}, bf16[256,1536]{1,0:T(8,128)(2,1)}, bf16[160,1024]{1,0:T(8,128)(2,1)}) custom-call(s32[24]{0:T(128)S(1)} %copy-done.26, s32[16]{0:T(128)S(1)} %stack.137.place_ref, f32[8,512]{1,0:T(8,128)S(1)} %squeeze.41.gain_ref, bf16[256,512]{1,0:T(8,128)(2,1)S(1)} %add_convert_fusion.6.refs_0_, ...), custom_call_target="tpu_custom_call" | custom-call | flops 6442450944 | bytes 18874368 | tf_op jit(solution)/shard_map/pallas_call | solution.py:123
  285.1 7.6 %shard_map.86.inner = bf16[256,512]{1,0:T(8,128)(2,1)S(1)} custom-call(bf16[256,1536]{1,0:T(8,128)(2,1)S(1)} %copy-done.34, bf16[256,1536]{1,0:T(8,128)(2,1)S(1)} %copy-done.35, f32[9,512]{1,0:T(8,128)S(1)} %slice.158.feat_ref, f32[128,512]{1,0:T(8,128)S(1)} %slice.159.filter_ref, f32[1,512]{1,0:T(1,128)S(1)} %slice.160.skip_ref), custom_call_target="tpu_custom_call" | custom-call | flops 3221225472 | bytes 3145728 | tf_op jit(solution)/shard_map/pallas_call | solution.py:273
  292.7 7.6 %shard_map.87.inner = bf16[256,512]{1,0:T(8,128)(2,1)S(1)} custom-call(bf16[160,1024]{1,0:T(8,128)(2,1)S(1)} %collective-permute-done.48.before_ref, bf16[256,1536]{1,0:T(8,128)(2,1)S(1)} %copy-done.34, f32[9,512]{1,0:T(8,128)S(1)} %slice.158.feat_ref, f32[128,512]{1,0:T(8,128)S(1)} %slice.159.filter_ref, f32[1,512]{1,0:T(1,128)S(1)} %slice.160.skip_ref), custom_call_target="tpu_custom_call" | custom-call | flops 3221225472 | bytes 3145728 | tf_op jit(solution)/shard_map/pallas_call | solution.py:273
  300.4 4.1 %shard_map.88 = (bf16[4,256,512]{2,1,0:T(8,128)(2,1)S(1)}, bf16[4,256,512]{2,1,0:T(8,128)(2,1)S(1)}) custom-call(s32[24]{0:T(128)S(1)} %copy-done.26, bf16[256,512]{1,0:T(8,128)(2,1)S(1)} %shard_map.87.inner, bf16[16,512,256]{2,1,0:T(8,128)(2,1)} %bitcast.67), custom_call_target="tpu_custom_call" | custom-call | flops 1073741824 | bytes 6291456 | tf_op jit(solution)/shard_map/pallas_call | solution.py:296
  304.5 3.4 collective-permute-start.51
  307.8 4.1 %shard_map.89 = (bf16[4,256,512]{2,1,0:T(8,128)(2,1)S(1)}, bf16[4,256,512]{2,1,0:T(8,128)(2,1)S(1)}) custom-call(s32[24]{0:T(128)S(1)} %copy-done.26, bf16[256,512]{1,0:T(8,128)(2,1)S(1)} %shard_map.86.inner, bf16[16,512,256]{2,1,0:T(8,128)(2,1)} %bitcast.68), custom_call_target="tpu_custom_call" | custom-call | flops 1073741824 | bytes 6291456 | tf_op jit(solution)/shard_map/pallas_call | solution.py:296
  313.8 4.3 %collective-permute-start.53 = (bf16[256,512]{1,0:T(8,128)(2,1)S(1)}, bf16[256,512]{1,0:T(8,128)(2,1)S(1)}, u32[]{:S(2)}, u32[]{:S(2)}) collective-permute-start(bf16[256,512]{1,0:T(8,128)(2,1)S(1)} %get-tuple-element.133), channel_id=1, source_target_pairs={{0,6},{1,14},{2,0},{3,8},{4,2},{5,10},{6,4},{7,12},{8,7},{9,15},{1... | collective-permute-start | bytes 786440 | tf_op jit(solution)/shard_map/ppermute | solution.py:31
  319.3 3.1 collective-permute-start.55
  322.9 3.6 %collective-permute-start.57 = (bf16[256,512]{1,0:T(8,128)(2,1)S(1)}, bf16[256,512]{1,0:T(8,128)(2,1)S(1)}, u32[]{:S(2)}, u32[]{:S(2)}) collective-permute-start(bf16[256,512]{1,0:T(8,128)(2,1)S(1)} %get-tuple-element.138), channel_id=1, source_target_pairs={{0,2},{1,10},{2,4},{3,12},{4,6},{5,14},{6,0},{7,8},{8,3},{9,11},{1... | collective-permute-start | bytes 786440 | tf_op jit(solution)/shard_map/ppermute | solution.py:31
  326.5 1.8 collective-permute-start.58
  328.3 3.7 %collective-permute-start.59 = (bf16[256,512]{1,0:T(8,128)(2,1)S(1)}, bf16[256,512]{1,0:T(8,128)(2,1)S(1)}, u32[]{:S(2)}, u32[]{:S(2)}) collective-permute-start(bf16[256,512]{1,0:T(8,128)(2,1)S(1)} %get-tuple-element.136), channel_id=1, source_target_pairs={{0,4},{1,12},{2,6},{3,14},{4,0},{5,8},{6,2},{7,10},{8,5},{9,13},{1... | collective-permute-start | bytes 786440 | tf_op jit(solution)/shard_map/ppermute | solution.py:31
  332.0 3.4 collective-permute-start.60
  336.5 3.9 %collective-permute-done.59 = bf16[256,512]{1,0:T(8,128)(2,1)S(1)} collective-permute-done((bf16[256,512]{1,0:T(8,128)(2,1)S(1)}, bf16[256,512]{1,0:T(8,128)(2,1)S(1)}, u32[]{:S(2)}, u32[]{:S(2)}) %collective-permute-start.59) | collective-permute-done | bytes 262176 | tf_op jit(solution)/shard_map/ppermute | solution.py:31
  (241 shorter events, 68.6 us)
Async XLA Ops:
  6.5 110.1 %all-gather.7.cloned.1.call-start = ((), (), s32[]{:S(2)}) async-start(), calls=%async_computation | async-start | bytes 4718592 | tf_op jit(solution)/shard_map/all_gather | solution.py:317
  7.3 255.8 %all-gather.9.cloned.1.call-start = ((), (), s32[]{:S(2)}) async-start(), calls=%async_computation.1 | async-start | bytes 13369344 | tf_op jit(solution)/shard_map/all_gather | solution.py:313
  10.0 30.2 %collective-permute-start.1 = (bf16[256,2048]{1,0:T(8,128)(2,1)S(1)}, bf16[256,2048]{1,0:T(8,128)(2,1)S(1)}, u32[]{:S(2)}, u32[]{:S(2)}) collective-permute-start(bf16[256,2048]{1,0:T(8,128)(2,1)S(1)} %pad_maximum_fusion.1.refs_1_.refs_0_), channel_id=1, source_target_pairs={{0,64},{64,0},{1,65},{65,1},{2,66},{66,2},{3,67},{67,3},{4,68},{68... | collective-permute-start | bytes 3145736 | tf_op jit(solution)/shard_map/ppermute | solution.py:20
  13.3 39.2 %collective-permute-start.2 = (bf16[256,3,512]{0,2,1:T(8,128)(2,1)}, bf16[256,3,512]{0,2,1:T(8,128)(2,1)}, u32[]{:S(2)}, u32[]{:S(2)}) collective-permute-start(bf16[256,3,512]{0,2,1:T(8,128)(2,1)} %bitcast.31), channel_id=1, source_target_pairs={{1,8},{8,1},{3,10},{10,3},{5,12},{12,5},{7,14},{14,7},{17,24},{24,... | collective-permute-start | bytes 2359304 | tf_op jit(solution)/shard_map/ppermute | solution.py:24
  18.5 37.5 %collective-permute-start.4 = (bf16[256,2048]{1,0:T(8,128)(2,1)S(1)}, bf16[256,2048]{1,0:T(8,128)(2,1)S(1)}, u32[]{:S(2)}, u32[]{:S(2)}) collective-permute-start(bf16[256,2048]{1,0:T(8,128)(2,1)S(1)} %pad_maximum_fusion.1.refs_1_.refs_0_), channel_id=1, source_target_pairs={{0,16},{16,32},{32,48},{48,0},{1,17},{17,33},{33,49},{49,1},{2,18}... | collective-permute-start | bytes 3145736 | tf_op jit(solution)/shard_map/ppermute | solution.py:20
  19.8 36.2 %collective-permute-start.5 = (bf16[256,2048]{1,0:T(8,128)(2,1)S(1)}, bf16[256,2048]{1,0:T(8,128)(2,1)}, u32[]{:S(2)}, u32[]{:S(2)}) collective-permute-start(bf16[256,2048]{1,0:T(8,128)(2,1)S(1)} %pad_maximum_fusion.1.refs_1_.refs_0_), channel_id=1, source_target_pairs={{0,48},{16,0},{32,16},{48,32},{1,49},{17,1},{33,17},{49,33},{2,50}... | collective-permute-start | bytes 3145736 | tf_op jit(solution)/shard_map/ppermute | solution.py:20
  21.3 45.1 %collective-permute-start.6 = (bf16[256,2048]{1,0:T(8,128)(2,1)S(1)}, bf16[256,2048]{1,0:T(8,128)(2,1)}, u32[]{:S(2)}, u32[]{:S(2)}) collective-permute-start(bf16[256,2048]{1,0:T(8,128)(2,1)S(1)} %pad_maximum_fusion.1.refs_1_.refs_0_), channel_id=1, source_target_pairs={{0,32},{16,48},{32,0},{48,16},{1,33},{17,49},{33,1},{49,17},{2,34}... | collective-permute-start | bytes 3145736 | tf_op jit(solution)/shard_map/ppermute | solution.py:20
  40.2 15.0 %collective-permute-start.3 = (bf16[512,256]{1,0:T(8,128)(2,1)S(1)}, bf16[512,256]{1,0:T(8,128)(2,1)S(1)}, u32[]{:S(2)}, u32[]{:S(2)}) collective-permute-start(bf16[512,256]{1,0:T(8,128)(2,1)S(1)} %slice_bitcast_fusion.11), channel_id=1, source_target_pairs={{1,8},{8,1},{3,10},{10,3},{5,12},{12,5},{7,14},{14,7},{17,24},{24,... | collective-permute-start | bytes 786440 | tf_op jit(solution)/shard_map/ppermute | solution.py:24
  67.8 36.0 %collective-permute-start.7 = (bf16[3,256,768]{2,1,0:T(8,128)(2,1)S(1)}, bf16[3,256,768]{2,1,0:T(8,128)(2,1)S(1)}, u32[]{:S(2)}, u32[]{:S(2)}) collective-permute-start(bf16[3,256,768]{2,1,0:T(8,128)(2,1)S(1)} %pad_maximum_fusion), channel_id=1, source_target_pairs={{0,64},{64,0},{1,65},{65,1},{2,66},{66,2},{3,67},{67,3},{4,68},{68... | collective-permute-start | bytes 3538952 | tf_op jit(solution)/shard_map/ppermute | solution.py:20
  68.0 17.7 %collective-permute-start.8 = (bf16[256,1280]{1,0:T(8,128)(2,1)S(1)}, bf16[256,1280]{1,0:T(8,128)(2,1)S(1)}, u32[]{:S(2)}, u32[]{:S(2)}) collective-permute-start(bf16[256,1280]{1,0:T(8,128)(2,1)S(1)} %slice.131), channel_id=1, source_target_pairs={{0,16},{16,32},{32,48},{48,0},{1,17},{17,33},{33,49},{49,1},{2,18}... | collective-permute-start | bytes 1966088 | tf_op jit(solution)/shard_map/ppermute | solution.py:20
  69.4 30.1 %collective-permute-start.10 = (bf16[256,1280]{1,0:T(8,128)(2,1)S(1)}, bf16[256,1280]{1,0:T(8,128)(2,1)S(1)}, u32[]{:S(2)}, u32[]{:S(2)}) collective-permute-start(bf16[256,1280]{1,0:T(8,128)(2,1)S(1)} %slice.131), channel_id=1, source_target_pairs={{0,32},{16,48},{32,0},{48,16},{1,33},{17,49},{33,1},{49,17},{2,34}... | collective-permute-start | bytes 1966088 | tf_op jit(solution)/shard_map/ppermute | solution.py:20
  71.1 29.2 %collective-permute-start.9 = (bf16[256,1280]{1,0:T(8,128)(2,1)S(1)}, bf16[256,1280]{1,0:T(8,128)(2,1)S(1)}, u32[]{:S(2)}, u32[]{:S(2)}) collective-permute-start(bf16[256,1280]{1,0:T(8,128)(2,1)S(1)} %slice.131), channel_id=1, source_target_pairs={{0,48},{16,0},{32,16},{48,32},{1,49},{17,1},{33,17},{49,33},{2,50}... | collective-permute-start | bytes 1966088 | tf_op jit(solution)/shard_map/ppermute | solution.py:20
  85.6 18.3 %collective-permute-start.15 = (bf16[256,2048]{1,0:T(8,128)(2,1)}, bf16[256,2048]{1,0:T(8,128)(2,1)S(1)}, u32[]{:S(2)}, u32[]{:S(2)}) collective-permute-start(bf16[256,2048]{1,0:T(8,128)(2,1)} %collective-permute-done.6.refs_5_.refs_4_), channel_id=1, source_target_pairs={{0,8},{8,0},{1,9},{9,1},{2,10},{10,2},{3,11},{11,3},{4,12},{12,4},... | collective-permute-start | bytes 3145736 | tf_op jit(solution)/shard_map/ppermute | solution.py:20
  85.7 18.3 %collective-permute-start.14 = (bf16[256,2048]{1,0:T(8,128)(2,1)}, bf16[256,2048]{1,0:T(8,128)(2,1)S(1)}, u32[]{:S(2)}, u32[]{:S(2)}) collective-permute-start(bf16[256,2048]{1,0:T(8,128)(2,1)} %collective-permute-done.5.refs_4_.refs_3_), channel_id=1, source_target_pairs={{0,8},{8,0},{1,9},{9,1},{2,10},{10,2},{3,11},{11,3},{4,12},{12,4},... | collective-permute-start | bytes 3145736 | tf_op jit(solution)/shard_map/ppermute | solution.py:20
  109.8 190.6 %all-gather.11.cloned.1.call-start = ((), (), s32[]{:S(2)}) async-start(), calls=%async_computation.2 | async-start | bytes 4456448 | tf_op jit(solution)/shard_map/all_gather | solution.py:313
  140.6 19.7 %collective-permute-start.24 = (bf16[256,1024]{1,0:T(8,128)(2,1)}, bf16[256,1024]{1,0:T(8,128)(2,1)}, u32[]{:S(2)}, u32[]{:S(2)}) collective-permute-start(bf16[256,1024]{1,0:T(8,128)(2,1)} %get-tuple-element.92), channel_id=1, source_target_pairs={{0,2},{2,4},{4,6},{6,0},{1,3},{3,5},{5,7},{7,1},{8,10},{10,12},{12... | collective-permute-start | bytes 1572872 | tf_op jit(solution)/shard_map/ppermute | solution.py:20
  142.0 20.5 %collective-permute-start.25 = (bf16[256,1024]{1,0:T(8,128)(2,1)}, bf16[256,1024]{1,0:T(8,128)(2,1)}, u32[]{:S(2)}, u32[]{:S(2)}) collective-permute-start(bf16[256,1024]{1,0:T(8,128)(2,1)} %get-tuple-element.93), channel_id=1, source_target_pairs={{0,6},{2,0},{4,2},{6,4},{1,7},{3,1},{5,3},{7,5},{8,14},{10,8},{12,... | collective-permute-start | bytes 1572872 | tf_op jit(solution)/shard_map/ppermute | solution.py:20
  143.5 24.5 %collective-permute-start.26 = (bf16[256,1024]{1,0:T(8,128)(2,1)}, bf16[256,1024]{1,0:T(8,128)(2,1)}, u32[]{:S(2)}, u32[]{:S(2)}) collective-permute-start(bf16[256,1024]{1,0:T(8,128)(2,1)} %get-tuple-element.94), channel_id=1, source_target_pairs={{0,4},{2,6},{4,0},{6,2},{1,5},{3,7},{5,1},{7,3},{8,12},{10,14},{12... | collective-permute-start | bytes 1572872 | tf_op jit(solution)/shard_map/ppermute | solution.py:20
  150.3 25.9 %collective-permute-start = (bf16[512,512]{1,0:T(8,128)(2,1)S(1)}, bf16[512,512]{1,0:T(8,128)(2,1)S(1)}, u32[]{:S(2)}, u32[]{:S(2)}) collective-permute-start(bf16[512,512]{1,0:T(8,128)(2,1)S(1)} %dynamic-slice_bitcast_fusion), channel_id=1, source_target_pairs={{0,8},{8,0},{1,9},{9,1},{2,10},{10,2},{3,11},{11,3},{4,12},{12,4},... | collective-permute-start | bytes 1572872 | tf_op jit(solution)/shard_map/ppermute | solution.py:20
  159.7 20.8 %collective-permute-start.21 = (bf16[256,1024]{1,0:T(8,128)(2,1)S(1)}, bf16[256,1024]{1,0:T(8,128)(2,1)S(1)}, u32[]{:S(2)}, u32[]{:S(2)}) collective-permute-start(bf16[256,1024]{1,0:T(8,128)(2,1)S(1)} %get-tuple-element.87), channel_id=1, source_target_pairs={{0,2},{2,4},{4,6},{6,0},{1,3},{3,5},{5,7},{7,1},{8,10},{10,12},{12... | collective-permute-start | bytes 1572872 | tf_op jit(solution)/shard_map/ppermute | solution.py:20
  160.3 25.0 %collective-permute-start.22 = (bf16[256,1024]{1,0:T(8,128)(2,1)S(1)}, bf16[256,1024]{1,0:T(8,128)(2,1)S(1)}, u32[]{:S(2)}, u32[]{:S(2)}) collective-permute-start(bf16[256,1024]{1,0:T(8,128)(2,1)S(1)} %get-tuple-element.88), channel_id=1, source_target_pairs={{0,6},{2,0},{4,2},{6,4},{1,7},{3,1},{5,3},{7,5},{8,14},{10,8},{12,... | collective-permute-start | bytes 1572872 | tf_op jit(solution)/shard_map/ppermute | solution.py:20
  162.5 27.8 %collective-permute-start.23 = (bf16[256,1024]{1,0:T(8,128)(2,1)S(1)}, bf16[256,1024]{1,0:T(8,128)(2,1)S(1)}, u32[]{:S(2)}, u32[]{:S(2)}) collective-permute-start(bf16[256,1024]{1,0:T(8,128)(2,1)S(1)} %get-tuple-element.89), channel_id=1, source_target_pairs={{0,4},{2,6},{4,0},{6,2},{1,5},{3,7},{5,1},{7,3},{8,12},{10,14},{12... | collective-permute-start | bytes 1572872 | tf_op jit(solution)/shard_map/ppermute | solution.py:20
  169.8 24.4 %collective-permute-start.28 = (bf16[256,512]{1,0:T(8,128)(2,1)S(1)}, bf16[256,512]{1,0:T(8,128)(2,1)S(1)}, u32[]{:S(2)}, u32[]{:S(2)}) collective-permute-start(bf16[256,512]{1,0:T(8,128)(2,1)S(1)} %get-tuple-element.141), channel_id=1, source_target_pairs={{1,8},{8,1},{3,10},{10,3},{5,12},{12,5},{7,14},{14,7},{17,24},{24,... | collective-permute-start | bytes 786440 | tf_op jit(solution)/shard_map/ppermute | solution.py:377
  176.2 17.9 %collective-permute-start.29 = (bf16[256,512]{1,0:T(8,128)(2,1)S(1)}, bf16[256,512]{1,0:T(8,128)(2,1)S(1)}, u32[]{:S(2)}, u32[]{:S(2)}) collective-permute-start(bf16[256,512]{1,0:T(8,128)(2,1)S(1)} %get-tuple-element.141), channel_id=1, source_target_pairs={{0,8},{9,1},{2,10},{11,3},{4,12},{13,5},{6,14},{15,7},{16,24},{25,... | collective-permute-start | bytes 786440 | tf_op jit(solution)/shard_map/ppermute | solution.py:378
  180.5 13.6 %collective-permute-start.27 = (bf16[256,512]{1,0:T(8,128)(2,1)S(1)}, bf16[256,512]{1,0:T(8,128)(2,1)S(1)}, u32[]{:S(2)}, u32[]{:S(2)}) collective-permute-start(bf16[256,512]{1,0:T(8,128)(2,1)S(1)} %get-tuple-element.142), channel_id=1, source_target_pairs={{1,0},{8,9},{3,2},{10,11},{5,4},{12,13},{7,6},{14,15},{17,16},{24,... | collective-permute-start | bytes 786440 | tf_op jit(solution)/shard_map/ppermute | solution.py:376
  196.0 21.7 %collective-permute-start.31 = (bf16[256,512]{1,0:T(8,128)(2,1)S(1)}, bf16[256,512]{1,0:T(8,128)(2,1)S(1)}, u32[]{:S(2)}, u32[]{:S(2)}) collective-permute-start(bf16[256,512]{1,0:T(8,128)(2,1)S(1)} %get-tuple-element.139), channel_id=1, source_target_pairs={{1,8},{8,1},{3,10},{10,3},{5,12},{12,5},{7,14},{14,7},{17,24},{24,... | collective-permute-start | bytes 786440 | tf_op jit(solution)/shard_map/ppermute | solution.py:377
  199.0 18.7 %collective-permute-start.30 = (bf16[256,512]{1,0:T(8,128)(2,1)S(1)}, bf16[256,512]{1,0:T(8,128)(2,1)S(1)}, u32[]{:S(2)}, u32[]{:S(2)}) collective-permute-start(bf16[256,512]{1,0:T(8,128)(2,1)S(1)} %get-tuple-element.140), channel_id=1, source_target_pairs={{1,0},{8,9},{3,2},{10,11},{5,4},{12,13},{7,6},{14,15},{17,16},{24,... | collective-permute-start | bytes 786440 | tf_op jit(solution)/shard_map/ppermute | solution.py:376
  202.7 15.1 %collective-permute-start.33 = (bf16[256,512]{1,0:T(8,128)(2,1)S(1)}, bf16[256,512]{1,0:T(8,128)(2,1)S(1)}, u32[]{:S(2)}, u32[]{:S(2)}) collective-permute-start(bf16[256,512]{1,0:T(8,128)(2,1)S(1)} %add_convert_fusion.7.refs_8_), channel_id=1, source_target_pairs={{0,2},{2,4},{4,6},{6,0},{1,3},{3,5},{5,7},{7,1},{8,10},{10,12},{12... | collective-permute-start | bytes 786440 | tf_op jit(solution)/shard_map/ppermute | solution.py:20
  203.3 14.4 %collective-permute-start.34 = (bf16[256,512]{1,0:T(8,128)(2,1)S(1)}, bf16[256,512]{1,0:T(8,128)(2,1)S(1)}, u32[]{:S(2)}, u32[]{:S(2)}) collective-permute-start(bf16[256,512]{1,0:T(8,128)(2,1)S(1)} %add_convert_fusion.7.refs_8_), channel_id=1, source_target_pairs={{0,6},{2,0},{4,2},{6,4},{1,7},{3,1},{5,3},{7,5},{8,14},{10,8},{12,... | collective-permute-start | bytes 786440 | tf_op jit(solution)/shard_map/ppermute | solution.py:20
  205.4 20.3 %collective-permute-start.35 = (bf16[256,512]{1,0:T(8,128)(2,1)S(1)}, bf16[256,512]{1,0:T(8,128)(2,1)S(1)}, u32[]{:S(2)}, u32[]{:S(2)}) collective-permute-start(bf16[256,512]{1,0:T(8,128)(2,1)S(1)} %add_convert_fusion.7.refs_8_), channel_id=1, source_target_pairs={{0,4},{2,6},{4,0},{6,2},{1,5},{3,7},{5,1},{7,3},{8,12},{10,14},{12... | collective-permute-start | bytes 786440 | tf_op jit(solution)/shard_map/ppermute | solution.py:20
  225.9 14.5 %collective-permute-start.36 = (bf16[256,512]{1,0:T(8,128)(2,1)S(1)}, bf16[256,512]{1,0:T(8,128)(2,1)S(1)}, u32[]{:S(2)}, u32[]{:S(2)}) collective-permute-start(bf16[256,512]{1,0:T(8,128)(2,1)S(1)} %add_convert_fusion.6.refs_0_), channel_id=1, source_target_pairs={{0,2},{2,4},{4,6},{6,0},{1,3},{3,5},{5,7},{7,1},{8,10},{10,12},{12... | collective-permute-start | bytes 786440 | tf_op jit(solution)/shard_map/ppermute | solution.py:20
  226.0 14.7 %collective-permute-start.37 = (bf16[256,512]{1,0:T(8,128)(2,1)S(1)}, bf16[256,512]{1,0:T(8,128)(2,1)S(1)}, u32[]{:S(2)}, u32[]{:S(2)}) collective-permute-start(bf16[256,512]{1,0:T(8,128)(2,1)S(1)} %add_convert_fusion.6.refs_0_), channel_id=1, source_target_pairs={{0,6},{2,0},{4,2},{6,4},{1,7},{3,1},{5,3},{7,5},{8,14},{10,8},{12,... | collective-permute-start | bytes 786440 | tf_op jit(solution)/shard_map/ppermute | solution.py:20
  228.6 12.3 %collective-permute-start.38 = (bf16[256,512]{1,0:T(8,128)(2,1)S(1)}, bf16[256,512]{1,0:T(8,128)(2,1)S(1)}, u32[]{:S(2)}, u32[]{:S(2)}) collective-permute-start(bf16[256,512]{1,0:T(8,128)(2,1)S(1)} %add_convert_fusion.6.refs_0_), channel_id=1, source_target_pairs={{0,4},{2,6},{4,0},{6,2},{1,5},{3,7},{5,1},{7,3},{8,12},{10,14},{12... | collective-permute-start | bytes 786440 | tf_op jit(solution)/shard_map/ppermute | solution.py:20
  228.7 16.7 %collective-permute-start.47 = (f32[138,512]{1,0:T(8,128)S(1)}, f32[138,512]{1,0:T(8,128)}, u32[]{:S(2)}, u32[]{:S(2)}) collective-permute-start(f32[138,512]{1,0:T(8,128)S(1)} %pad_maximum_fusion.3), channel_id=1, source_target_pairs={{1,8},{8,1},{3,10},{10,3},{5,12},{12,5},{7,14},{14,7},{17,24},{24,... | collective-permute-start | bytes 847880 | tf_op jit(solution)/shard_map/ppermute | solution.py:24
  242.7 14.7 %collective-permute-start.50 = (bf16[256,512]{1,0:T(8,128)(2,1)S(1)}, bf16[256,512]{1,0:T(8,128)(2,1)}, u32[]{:S(2)}, u32[]{:S(2)}) collective-permute-start(bf16[256,512]{1,0:T(8,128)(2,1)S(1)} %add_convert_fusion.6.refs_0_), channel_id=1, source_target_pairs={{1,8},{8,1},{3,10},{10,3},{5,12},{12,5},{7,14},{14,7},{17,24},{24,... | collective-permute-start | bytes 786440 | tf_op jit(solution)/shard_map/ppermute | solution.py:24
  244.8 16.2 %collective-permute-start.43 = (bf16[256,512]{1,0:T(8,128)(2,1)S(1)}, bf16[256,512]{1,0:T(8,128)(2,1)S(1)}, u32[]{:S(2)}, u32[]{:S(2)}) collective-permute-start(bf16[256,512]{1,0:T(8,128)(2,1)S(1)} %add_convert_fusion.7.refs_8_), channel_id=1, source_target_pairs={{0,8},{8,0},{1,9},{9,1},{2,10},{10,2},{3,11},{11,3},{4,12},{12,4},... | collective-permute-start | bytes 786440 | tf_op jit(solution)/shard_map/ppermute | solution.py:20
  244.9 16.8 %collective-permute-start.44 = (bf16[256,512]{1,0:T(8,128)(2,1)S(1)}, bf16[256,512]{1,0:T(8,128)(2,1)S(1)}, u32[]{:S(2)}, u32[]{:S(2)}) collective-permute-start(bf16[256,512]{1,0:T(8,128)(2,1)S(1)} %collective-permute-done.33.refs_9_), channel_id=1, source_target_pairs={{0,8},{8,0},{1,9},{9,1},{2,10},{10,2},{3,11},{11,3},{4,12},{12,4},... | collective-permute-start | bytes 786440 | tf_op jit(solution)/shard_map/ppermute | solution.py:20
  245.4 17.0 %collective-permute-start.45 = (bf16[256,512]{1,0:T(8,128)(2,1)S(1)}, bf16[256,512]{1,0:T(8,128)(2,1)S(1)}, u32[]{:S(2)}, u32[]{:S(2)}) collective-permute-start(bf16[256,512]{1,0:T(8,128)(2,1)S(1)} %collective-permute-done.34.refs_10_), channel_id=1, source_target_pairs={{0,8},{8,0},{1,9},{9,1},{2,10},{10,2},{3,11},{11,3},{4,12},{12,4},... | collective-permute-start | bytes 786440 | tf_op jit(solution)/shard_map/ppermute | solution.py:20
  245.4 17.6 %collective-permute-start.46 = (bf16[256,512]{1,0:T(8,128)(2,1)S(1)}, bf16[256,512]{1,0:T(8,128)(2,1)}, u32[]{:S(2)}, u32[]{:S(2)}) collective-permute-start(bf16[256,512]{1,0:T(8,128)(2,1)S(1)} %collective-permute-done.35.refs_11_), channel_id=1, source_target_pairs={{0,8},{8,0},{1,9},{9,1},{2,10},{10,2},{3,11},{11,3},{4,12},{12,4},... | collective-permute-start | bytes 786440 | tf_op jit(solution)/shard_map/ppermute | solution.py:20
  257.3 24.5 %collective-permute-start.49 = (bf16[256,512]{1,0:T(8,128)(2,1)S(1)}, bf16[256,512]{1,0:T(8,128)(2,1)}, u32[]{:S(2)}, u32[]{:S(2)}) collective-permute-start(bf16[256,512]{1,0:T(8,128)(2,1)S(1)} %add_convert_fusion.7.refs_8_), channel_id=1, source_target_pairs={{1,8},{8,1},{3,10},{10,3},{5,12},{12,5},{7,14},{14,7},{17,24},{24,... | collective-permute-start | bytes 786440 | tf_op jit(solution)/shard_map/ppermute | solution.py:24
  280.5 12.2 %collective-permute-start.48 = (bf16[160,1024]{1,0:T(8,128)(2,1)}, bf16[160,1024]{1,0:T(8,128)(2,1)S(1)}, u32[]{:S(2)}, u32[]{:S(2)}) collective-permute-start(bf16[160,1024]{1,0:T(8,128)(2,1)} %get-tuple-element.113), channel_id=1, source_target_pairs={{0,1},{1,16},{16,17},{17,32},{32,33},{33,48},{48,49},{49,64},{64,6... | collective-permute-start | bytes 983048 | tf_op jit(solution)/shard_map/ppermute | solution.py:35
  311.9 10.5 %collective-permute-start.56 = (bf16[4,256,512]{2,1,0:T(8,128)(2,1)S(1)}, bf16[4,256,512]{2,1,0:T(8,128)(2,1)S(1)}, u32[]{:S(2)}, u32[]{:S(2)}) collective-permute-start(bf16[4,256,512]{2,1,0:T(8,128)(2,1)S(1)} %get-tuple-element.124), channel_id=1, source_target_pairs={{0,8},{8,0},{1,9},{9,1},{2,10},{10,2},{3,11},{11,3},{4,12},{12,4},... | collective-permute-start | bytes 3145736 | tf_op jit(solution)/shard_map/ppermute | solution.py:20
  312.7 13.8 %collective-permute-start.52 = (bf16[256,512]{1,0:T(8,128)(2,1)S(1)}, bf16[256,512]{1,0:T(8,128)(2,1)S(1)}, u32[]{:S(2)}, u32[]{:S(2)}) collective-permute-start(bf16[256,512]{1,0:T(8,128)(2,1)S(1)} %get-tuple-element.134), channel_id=1, source_target_pairs={{0,2},{1,10},{2,4},{3,12},{4,6},{5,14},{6,0},{7,8},{8,3},{9,11},{1... | collective-permute-start | bytes 786440 | tf_op jit(solution)/shard_map/ppermute | solution.py:31
  313.8 14.5 %collective-permute-start.53 = (bf16[256,512]{1,0:T(8,128)(2,1)S(1)}, bf16[256,512]{1,0:T(8,128)(2,1)S(1)}, u32[]{:S(2)}, u32[]{:S(2)}) collective-permute-start(bf16[256,512]{1,0:T(8,128)(2,1)S(1)} %get-tuple-element.133), channel_id=1, source_target_pairs={{0,6},{1,14},{2,0},{3,8},{4,2},{5,10},{6,4},{7,12},{8,7},{9,15},{1... | collective-permute-start | bytes 786440 | tf_op jit(solution)/shard_map/ppermute | solution.py:31
  318.1 13.9 %collective-permute-start.54 = (bf16[256,512]{1,0:T(8,128)(2,1)S(1)}, bf16[256,512]{1,0:T(8,128)(2,1)S(1)}, u32[]{:S(2)}, u32[]{:S(2)}) collective-permute-start(bf16[256,512]{1,0:T(8,128)(2,1)S(1)} %get-tuple-element.132), channel_id=1, source_target_pairs={{0,4},{1,12},{2,6},{3,14},{4,0},{5,8},{6,2},{7,10},{8,5},{9,13},{1... | collective-permute-start | bytes 786440 | tf_op jit(solution)/shard_map/ppermute | solution.py:31
  319.3 16.1 %collective-permute-start.55 = (bf16[256,512]{1,0:T(8,128)(2,1)S(1)}, bf16[256,512]{1,0:T(8,128)(2,1)S(1)}, u32[]{:S(2)}, u32[]{:S(2)}) collective-permute-start(bf16[256,512]{1,0:T(8,128)(2,1)S(1)} %get-tuple-element.131), channel_id=1, source_target_pairs={{1,8},{8,1},{3,10},{10,3},{5,12},{12,5},{7,14},{14,7},{17,24},{24,... | collective-permute-start | bytes 786440 | tf_op jit(solution)/shard_map/ppermute | solution.py:24
  322.9 12.8 %collective-permute-start.57 = (bf16[256,512]{1,0:T(8,128)(2,1)S(1)}, bf16[256,512]{1,0:T(8,128)(2,1)S(1)}, u32[]{:S(2)}, u32[]{:S(2)}) collective-permute-start(bf16[256,512]{1,0:T(8,128)(2,1)S(1)} %get-tuple-element.138), channel_id=1, source_target_pairs={{0,2},{1,10},{2,4},{3,12},{4,6},{5,14},{6,0},{7,8},{8,3},{9,11},{1... | collective-permute-start | bytes 786440 | tf_op jit(solution)/shard_map/ppermute | solution.py:31
  328.3 12.2 %collective-permute-start.59 = (bf16[256,512]{1,0:T(8,128)(2,1)S(1)}, bf16[256,512]{1,0:T(8,128)(2,1)S(1)}, u32[]{:S(2)}, u32[]{:S(2)}) collective-permute-start(bf16[256,512]{1,0:T(8,128)(2,1)S(1)} %get-tuple-element.136), channel_id=1, source_target_pairs={{0,4},{1,12},{2,6},{3,14},{4,0},{5,8},{6,2},{7,10},{8,5},{9,13},{1... | collective-permute-start | bytes 786440 | tf_op jit(solution)/shard_map/ppermute | solution.py:31
  (68 other events, 961.4 us)
Sparse Core Ops, SparseCore 0:
  9.7 89.0 all-gather.6
  109.9 98.0 all-gather.8
  210.1 59.0 all-gather.10
